TPU v7x, 32 devices: a whole 2x2x4 slice. The times are simulated.
32 devices in a mesh: rep: 16 (over z, y, x), sp: 2 (over core).
Axes of the slice: x: 2, y: 2, z: 4, core: 2. Of those that a mesh axis runs over, the one named last changes fastest.
Arguments:
- level_four: bfloat16 [16, 96, 96, 256], P('rep', 'sp'), may hold values from -25 to 25
- level_six: bfloat16 [16, 24, 24, 256], P('rep', 'sp'), may hold values from -25 to 25
- conv_weight: bfloat16 [9, 256, 256], replicated, may hold values from -0.125 to 0.125
- bn_gain: float32 [2, 256], replicated, may hold values from 0.1 to 1.9
- bn_shift: float32 [2, 256], replicated, may hold values from -3 to 3
- cotan_four: bfloat16 [16, 96, 96, 256], P('rep', 'sp'), may hold values from -6 to 6
- cotan_six: bfloat16 [16, 24, 24, 256], P('rep', 'sp'), may hold values from -6 to 6
Outputs:
- grad_four: bfloat16 [16, 96, 96, 256], P('rep', 'sp')
- grad_six: bfloat16 [16, 24, 24, 256], P('rep', 'sp')
- grad_weight: float32 [9, 256, 256], P(None, 'sp')
- grad_gain: float32 [2, 256], replicated
- grad_shift: float32 [2, 256], replicated
All inputs are finite; a program needn't handle non-finite values.
Results may differ from a plain program's by a relative error of at most 0.0052.
Values may be sent and summed in bfloat16 or wider, within the bound.
No kernel may reach another device: no remote copies, remote signals or barrier semaphores. Data moves between devices by JAX's collectives and lax.ppermute only.
A program may use at most 128 MiB of HBM per device.

v0:
```python
import functools

import jax
import jax.numpy as jnp
from jax import lax
from jax.experimental import pallas as pl
from jax.experimental.pallas import tpu as pltpu
from jax.sharding import PartitionSpec as P

GROUP = 16
RADIX = 4
FAR_FIRST = (3, 2, 1)
EPSILON = 1e-05
F32 = jnp.float32
BF16 = jnp.bfloat16
VMEM_LIMIT = 20 * 1024 * 1024
EDGE_LIMIT = 60 * 1024 * 1024


def chunk_of(rows, most, multiple=1):
    sizes = [size for size in range(1, most + 1) if rows % size == 0 and size % multiple == 0]
    return max(sizes) if sizes else rows


def pitch_of(cols):
    return -(-cols // 16) * 16


def chunks_of(rows, most, multiple=1):
    size = chunk_of(rows, most, multiple)
    return [(start, start + size) for start in range(0, rows, size)]


def widen(cells, pitch):
    cells = cells.astype(F32)
    extra = pitch - cells.shape[0]
    if extra:
        cells = jnp.concatenate([cells, jnp.zeros((extra, cells.shape[1]), F32)], 0)
    return cells


def put_three(three, row, cells, cols, turned):
    pitch, chan = cells.shape
    left, right = pltpu.roll(cells, 1, 0), pltpu.roll(cells, pitch - 1, 0)
    if pitch == cols:
        col = lax.broadcasted_iota(jnp.int32, (8, chan), 0)
        left = jnp.concatenate([jnp.where(col == 0, 0.0, left[:8]), left[8:]], 0)
        right = jnp.concatenate([right[:-8], jnp.where(col == 7, 0.0, right[-8:])], 0)
    parts = (right, cells, left) if turned else (left, cells, right)
    for place, part in enumerate(parts):
        three[row, :, place * chan : (place + 1) * chan] = part.astype(BF16)


def beside(three, starts, size):
    pitch, width = three.shape[1:]
    return jnp.concatenate([three[start : start + size].reshape(size * pitch, width) for start in starts], 1)


def edges_valid(sp_count):
    index = lax.axis_index("sp")
    return jnp.where(index > 0, 1.0, 0.0), jnp.where(index < sp_count - 1, 1.0, 0.0)


def level_coefs(moments, gain, shift, count):
    mean = moments[0:1] / count
    spread = moments[1:2] / count - mean * mean
    return mean, lax.rsqrt(spread + EPSILON), gain, shift


def slope_of(conv, cotan, coefs):
    mean, rstd, gain, shift = coefs
    centred = conv.astype(F32) - mean
    half = centred * (0.5 * rstd * gain) + 0.5 * shift
    turn = jnp.tanh(half)
    return centred, cotan.astype(F32) * ((1.0 + turn) * (1.0 + half * (1.0 - turn)))


def masked(cells, cols):
    if cells.shape[0] == cols:
        return cells
    col = lax.broadcasted_iota(jnp.int32, cells.shape, 0)
    return jnp.where(col < cols, cells, 0.0)


def staged(fills, dots):
    fills[0]()
    for index, dot in enumerate(dots):
        if index + 1 < len(fills):
            fills[index + 1]()
        dot()


def conv_rows(three, starts, size, w_ref):
    pitch, width = three.shape[1:]
    lhs = [beside(three, (start, start + 1, start + 2), size) for start in starts]
    lhs = jnp.concatenate(lhs, 0) if len(lhs) > 1 else lhs[0]
    conv = jnp.dot(lhs, w_ref[...].reshape(3 * width, -1), preferred_element_type=F32).astype(BF16)
    return conv.reshape(len(starts) * size, pitch, -1)


def add_moments(sums, conv, cols):
    chan = conv.shape[2]
    conv = conv.astype(F32)
    if conv.shape[1] != cols:
        conv = conv[:, :cols]
    conv = conv.reshape(-1, 8, chan)
    sums[0].append(jnp.sum(conv, 0))
    sums[1].append(jnp.sum(conv * conv, 0))


def folded(parts):
    total = parts[0]
    for part in parts[1:]:
        total = total + part
    return jnp.sum(total, 0, keepdims=True)


def inner_level(x_ref, w_ref, conv_ref, three, sums, most):
    rows, cols = x_ref.shape[:2]
    pitch = three.shape[1]

    def fill_row(row):
        put_three(three, row, widen(x_ref[row], pitch), cols, False)

    def dot(start, end):
        conv = conv_rows(three, (start,), end - start, w_ref)
        conv_ref[start:end] = conv
        add_moments(sums, conv, cols)

    inner = rows - 2
    count = max(1, inner // most)
    bounds = [index * inner // count for index in range(count + 1)]
    fills, dots, done = [], [], 0
    for start, end in zip(bounds[:-1], bounds[1:]):
        fills.append(lambda todo=range(done, end + 2): [fill_row(row) for row in todo])
        done = end + 2
        dots.append(functools.partial(dot, start, end))
    return fills, dots


def inner_kernel(four_ref, six_ref, w_ref, conv_four_ref, conv_six_ref, moments_ref, three_four, three_six):
    sums_four, sums_six = ([], []), ([], [])
    fills_six, dots_six = inner_level(six_ref, w_ref, conv_six_ref, three_six, sums_six, 10)
    fills_four, dots_four = inner_level(four_ref, w_ref, conv_four_ref, three_four, sums_four, 8)
    staged(fills_six + fills_four, dots_six + dots_four)
    moments_ref[...] = jnp.concatenate([folded(parts) for parts in sums_four + sums_six], 0)


def outer_level(x_ref, top, bottom, valid, w_ref, conv_ref, three, sums):
    rows, cols = x_ref.shape[:2]
    pitch = three.shape[1]
    for edge in range(2):
        put_three(three, edge, top(edge) * valid[0], cols, False)
        put_three(three, 2 + edge, widen(x_ref[edge], pitch), cols, False)
        put_three(three, 4 + edge, widen(x_ref[rows - 2 + edge], pitch), cols, False)
        put_three(three, 6 + edge, bottom(edge) * valid[1], cols, False)
    conv = conv_rows(three, (0, 4), 2, w_ref)
    conv_ref[...] = conv
    add_moments(sums, conv[1:3], cols)


def outer_kernel(
    sp_count, four_ref, six_ref, above_ref, below_ref, w_ref, inner_ref,
    conv_four_ref, conv_six_ref, moments_ref, three_four, three_six,
):
    cols_four = four_ref.shape[1]
    valid = edges_valid(sp_count)
    base, pitch_six = 3 * cols_four, three_six.shape[1]

    def reader(ref, start, pitch):
        return lambda edge: ref[start + edge * pitch : start + (edge + 1) * pitch].astype(F32)

    sums_four, sums_six = ([], []), ([], [])
    outer_level(
        six_ref, reader(above_ref, base, pitch_six), reader(below_ref, base, pitch_six), valid, w_ref,
        conv_six_ref, three_six, sums_six,
    )
    outer_level(
        four_ref, reader(above_ref, 0, cols_four), reader(below_ref, 0, cols_four), valid, w_ref,
        conv_four_ref, three_four, sums_four,
    )
    sums = [folded(parts) for parts in sums_four + sums_six]
    moments_ref[...] = inner_ref[...] + jnp.concatenate(sums, 0)


def turn_kernel(four_ref, six_ref, turned_ref):
    rows_four, cols_four, chan = four_ref.shape
    rows_six, cols_six = six_ref.shape[:2]
    pitch = pitch_of(cols_six)
    for start, end in chunks_of(rows_four, 8, 4):
        cells = four_ref[start:end].reshape((end - start) * cols_four, chan)
        turned_ref[:, start * cols_four : end * cols_four] = cells.T
    cells = six_ref[...].astype(F32)
    cells = jnp.concatenate([cells, jnp.zeros((rows_six, pitch - cols_six, chan), F32)], 1).astype(BF16)
    turned_ref[:, rows_four * cols_four :] = cells.reshape(rows_six * pitch, chan).T


def slope_level(inner_ref, outer_ref, cotan_ref, above, below, coefs, slope_ref):
    rows, cols, chan = cotan_ref.shape
    pitch = inner_ref.shape[1]

    def put(row, conv, cotan):
        centred, slope = slope_of(conv, widen(cotan, pitch), coefs)
        slope_ref[row] = slope
        return centred, slope

    def add(sums, pair):
        centred, slope = pair
        first = jnp.sum(slope.reshape(-1, 8, chan), 0)
        second = jnp.sum((slope * centred).reshape(-1, 8, chan), 0)
        return sums[0] + first, sums[1] + second

    def step(row, sums):
        return add(sums, put(row + 2, inner_ref[row], cotan_ref[row + 1]))

    put(0, outer_ref[0], above)
    put(rows + 1, outer_ref[3], below)
    zero = jnp.zeros((8, chan), F32)
    sums = add((zero, zero), put(1, outer_ref[1], cotan_ref[0]))
    sums = add(sums, put(rows, outer_ref[2], cotan_ref[rows - 1]))
    looped = (rows - 2) // 8 * 8
    if looped:
        sums = lax.fori_loop(0, looped, step, sums, unroll=8)
    for row in range(looped, rows - 2):
        sums = step(row, sums)
    first = 0.5 * jnp.sum(sums[0], 0, keepdims=True)
    return first, 0.5 * coefs[1] * jnp.sum(sums[1], 0, keepdims=True)


def slope_kernel(
    counts, inner_four_ref, inner_six_ref, outer_four_ref, outer_six_ref, cotan_four_ref, cotan_six_ref,
    above_ref, below_ref, moments_ref, gain_ref, shift_ref, slope_four_ref, slope_six_ref, slopes_ref,
):
    sums = ()
    cols_four = cotan_four_ref.shape[1]
    starts = (2 * cols_four, 3 * cols_four + 2 * inner_six_ref.shape[1])
    for level, (inner_ref, outer_ref, cotan_ref, slope_ref) in enumerate(
        (
            (inner_four_ref, outer_four_ref, cotan_four_ref, slope_four_ref),
            (inner_six_ref, outer_six_ref, cotan_six_ref, slope_six_ref),
        )
    ):
        pair = moments_ref[2 * level : 2 * level + 2]
        here = slice(level, level + 1)
        edge = slice(starts[level], starts[level] + inner_ref.shape[1])
        coefs = level_coefs(pair, gain_ref[here], shift_ref[here], counts[level])
        sums += slope_level(inner_ref, outer_ref, cotan_ref, above_ref[edge], below_ref[edge], coefs, slope_ref)
    slopes_ref[...] = jnp.concatenate(sums, 0)


def backward_level(cols, inner_ref, outer_ref, slope_ref, valid, coefs, slopes, count, three):
    rows = inner_ref.shape[0] + 2
    pitch = three.shape[1]
    mean, rstd, gain, shift = coefs
    lead = gain * rstd
    offset, factor = lead * (slopes[0:1] / count), lead * rstd * (slopes[1:2] / count)

    def fill_row(row):
        if 2 <= row < rows:
            conv = inner_ref[row - 2]
        else:
            conv = outer_ref[row if row < 2 else row - rows + 2]
        centred = conv.astype(F32) - mean
        dconv = masked((0.5 * lead) * slope_ref[row] - (offset + centred * factor), cols)
        if row == 0:
            dconv = dconv * valid[0]
        elif row == rows + 1:
            dconv = dconv * valid[1]
        put_three(three, row, dconv, cols, True)

    def block(start, end):
        return beside(three, (start + 2, start + 1, start), end - start)

    return fill_row, block


def backward_bounds(rows):
    bounds = [0, min(8, rows)]
    while bounds[-1] < rows:
        bounds.append(min(bounds[-1] + 16, rows))
    return bounds


def backward_kernel(
    counts, sp_count, cols, turned_ref, inner_four_ref, inner_six_ref, outer_four_ref, outer_six_ref,
    slope_four_ref, slope_six_ref, moments_ref, slopes_ref, gain_ref, shift_ref, three_four, three_six, own_ref, sent_ref, total,
):
    valid = edges_valid(sp_count)
    parts = []
    for level, inner_ref, outer_ref, slope_ref, three in (
        (0, inner_four_ref, outer_four_ref, slope_four_ref, three_four),
        (1, inner_six_ref, outer_six_ref, slope_six_ref, three_six),
    ):
        here = slice(level, level + 1)
        pair = slice(2 * level, 2 * level + 2)
        coefs = level_coefs(moments_ref[pair], gain_ref[here], shift_ref[here], counts[level])
        parts.append(
            backward_level(
                cols[level], inner_ref, outer_ref, slope_ref, valid, coefs, slopes_ref[pair], counts[level], three
            )
        )
    (fill_four, block_four), (fill_six, block_six) = parts
    rows_four, rows_six = three_four.shape[0] - 2, three_six.shape[0] - 2
    pitch = three_four.shape[1]
    bounds = backward_bounds(rows_four)

    def dot(start, end):
        first, last = start * pitch, end * pitch
        rhs = block_four(start, end)
        if end == rows_four:
            rhs = jnp.concatenate([rhs, block_six(0, rows_six)], 0)
            last = turned_ref.shape[1]
        term = jnp.dot(turned_ref[:, first:last], rhs, preferred_element_type=F32)
        total[...] = total[...] + term if start else term

    fills, dots, done = [], [], 0
    for start, end in zip(bounds[:-1], bounds[1:]):
        todo = [functools.partial(fill_four, row) for row in range(done, end + 2)]
        if end == rows_four:
            todo += [functools.partial(fill_six, row) for row in range(rows_six + 2)]
        fills.append(lambda todo=todo: [fill() for fill in todo])
        done = end + 2
        dots.append(functools.partial(dot, start, end))
    staged(fills, dots)
    share, chan = own_ref.shape[1:]
    for step in range(sp_count):
        begin = pl.multiple_of((lax.axis_index("sp") ^ step) * share, share)
        for tap in range(9):
            part = total[pl.ds(begin, share), tap * chan : (tap + 1) * chan]
            if step == 0:
                own_ref[tap] = part
            else:
                sent_ref[step - 1, tap] = part.astype(BF16)


def input_chunks(three, turned, grad, chunks, offset, sent=None):
    cols, chan = grad.shape[1:]
    pitch = three.shape[1]
    for index, (start, end) in enumerate(chunks):
        size = end - start
        lhs = beside(three, (start + 2, start + 1, start), size)
        term = jnp.dot(lhs, turned[...], preferred_element_type=F32)
        grad[start - offset : end - offset] = term.reshape(size, pitch, chan)[:, :cols].astype(BF16)
        if sent is not None:
            sent(index, start, end)


def input_first_kernel(chunks, three_four, w_ref, grad_ref, turned):
    chan = w_ref.shape[1]
    for tap in range(9):
        turned[tap * chan : (tap + 1) * chan] = w_ref[tap].T
    input_chunks(three_four, turned, grad_ref, chunks, 0)


def input_second_kernel(
    chunks, done, three_four, three_six, turned, first_ref, grad_four_ref, grad_six_ref,
    grad_four, grad_six, sem_first, sems_four, sems_six,
):
    copies = [pltpu.make_async_copy(first_ref, grad_four_ref.at[:done], sem_first)]
    copies[0].start()

    def sender(grad, grad_ref, offset, sems):
        def sent(index, start, end):
            copy = pltpu.make_async_copy(grad.at[start - offset : end - offset], grad_ref.at[start:end], sems.at[index])
            copy.start()
            copies.append(copy)

        return sent

    six_chunks = chunks_of(grad_six.shape[0], 12)
    input_chunks(three_six, turned, grad_six, six_chunks, 0, sender(grad_six, grad_six_ref, 0, sems_six))
    input_chunks(three_four, turned, grad_four, chunks, done, sender(grad_four, grad_four_ref, done, sems_four))
    for copy in copies:
        copy.wait()


def swap(array, axis, stride):
    count = lax.axis_size(axis)
    return lax.ppermute(array, axis, [(i, i ^ stride) for i in range(count)])


def edge_kernel(starts, four_ref, six_ref, cotan_four_ref, cotan_six_ref, *rest):
    outs, six_rows, sems = rest[:-2], rest[-2], rest[-1]
    rows_four, cols_four = four_ref.shape[:2]
    rows_six = six_ref.shape[0]
    pitch = pitch_of(six_ref.shape[1])
    copies = []
    for number, (start, out_ref) in enumerate(zip(starts, outs)):
        last = (1 - jnp.minimum(lax.axis_index("sp"), 1)) if start is None else start
        for part, (ref, row) in enumerate(
            (
                (four_ref, last * (rows_four - 2)),
                (four_ref, last * (rows_four - 2) + 1),
                (cotan_four_ref, last * (rows_four - 1)),
                (six_ref, last * (rows_six - 2)),
                (six_ref, last * (rows_six - 2) + 1),
                (cotan_six_ref, last * (rows_six - 1)),
            )
        ):
            if part < 3:
                target = out_ref.at[part * cols_four : (part + 1) * cols_four]
            else:
                target = six_rows.at[number, part - 3]
            copies.append(pltpu.make_async_copy(ref.at[row], target, sems.at[number, part]))
    for copy in copies:
        copy.start()
    for copy in copies:
        copy.wait()
    for number, out_ref in enumerate(outs):
        for part in range(3):
            begin = 3 * cols_four + part * pitch
            out_ref[begin : begin + pitch] = widen(six_rows[number, part], pitch).astype(BF16)


def edges(four, six, cotan_four, cotan_six):
    count = lax.axis_size("sp")
    starts = (None,) if count == 2 else (0, 1)
    length = 3 * four.shape[1] + 3 * pitch_of(six.shape[1])
    vmem = pl.BlockSpec(memory_space=pltpu.VMEM)
    hbm = pl.BlockSpec(memory_space=pltpu.HBM)
    outs = pl.pallas_call(
        functools.partial(edge_kernel, starts),
        out_shape=tuple(jax.ShapeDtypeStruct((length, four.shape[2]), BF16) for _ in starts),
        in_specs=[hbm] * 4,
        out_specs=tuple(vmem for _ in starts),
        scratch_shapes=[
            pltpu.VMEM((len(starts), 3) + six.shape[1:], BF16),
            pltpu.SemaphoreType.DMA((len(starts), 6)),
        ],
        compiler_params=pltpu.CompilerParams(vmem_limit_bytes=EDGE_LIMIT),
        name="edges",
    )(four, six, cotan_four, cotan_six)
    if count == 2:
        met = swap(outs[0], "sp", 1)
        return met, met
    above = lax.ppermute(outs[1], "sp", [(i, (i + 1) % count) for i in range(count)])
    below = lax.ppermute(outs[0], "sp", [((i + 1) % count, i) for i in range(count)])
    return above, below


def swap_across(array, axis, stride):
    count, sp_count = lax.axis_size("rep"), lax.axis_size("sp")
    rep_stride, sp_stride = (stride, 1) if axis == "rep" else (0, stride ^ 1)
    pairs = [
        (rep * sp_count + sp, (rep ^ rep_stride) * sp_count + (sp ^ sp_stride))
        for rep in range(count)
        for sp in range(sp_count)
    ]
    return lax.ppermute(array, ("rep", "sp"), pairs)


def group_sum(sums):
    sums = sums + swap(sums, "sp", 1)
    stride = 2
    while stride < lax.axis_size("sp"):
        sums = sums + swap_across(sums, "sp", stride)
        stride = 2 * stride
    stride = 1
    while stride < GROUP:
        met = [swap_across(sums, "rep", k * stride) for k in FAR_FIRST]
        sums = (sums + met[2]) + (met[1] + met[0])
        stride = RADIX * stride
    return sums


def every_group(sums):
    stride = GROUP
    while stride < lax.axis_size("rep"):
        sums = sums + swap(sums, "rep", stride)
        stride = 2 * stride
    return sums


def places():
    digit = lax.axis_index("rep") & (RADIX - 1)
    return [digit ^ k for k in range(RADIX)]


def piece_of(pieces, index):
    sizes = (1,) + pieces.shape[1:]
    return lax.dynamic_slice(pieces, (index, 0, 0), sizes, allow_negative_indices=False)[0]


def scatter_start(own, sent, place):
    met = [swap(sent[step], "sp", step + 1) for step in range(sent.shape[0])]
    chan = own.shape[2]
    parts = [part.reshape(RADIX, -1, chan) for part in [own] + met]

    def piece(k):
        total = piece_of(parts[0], place[k])
        for part in parts[1:]:
            total = total + piece_of(part, place[k]).astype(F32)
        return total

    return piece(0), [piece(k).astype(BF16) for k in FAR_FIRST]


def added(own, met):
    return (own + met[2].astype(F32)) + (met[1].astype(F32) + met[0].astype(F32))


def fours(pieces, stride):
    return [swap(piece, "rep", k * stride) for k, piece in zip(FAR_FIRST, pieces)]


def swap_mixed(array, even, odd):
    count, sp_count = lax.axis_size("rep"), lax.axis_size("sp")
    pairs = [
        (rep * sp_count + sp, (rep ^ (odd if sp % 2 else even)) * sp_count + sp)
        for rep in range(count)
        for sp in range(sp_count)
    ]
    return lax.ppermute(array, ("rep", "sp"), pairs)


def both(own, met):
    return (own.astype(F32) + met.astype(F32)).astype(BF16)


def weight_gather(total, found):
    chan = total.shape[1]
    stride = GROUP
    while stride < lax.axis_size("rep"):
        total = added(total.astype(F32), fours([total] * 3, stride)).astype(BF16)
        stride = RADIX * stride
    met = [total] + fours([total] * 3, 1)[::-1]
    whole = jnp.zeros((RADIX,) + total.shape, F32)
    for k in (0,) + FAR_FIRST:
        start = (found[k], 0, 0)
        whole = lax.dynamic_update_slice(whole, met[k][None].astype(F32), start, allow_negative_indices=False)
    return whole


def local(level_four, level_six, conv_weight, bn_gain, bn_shift, cotan_four, cotan_six):
    sp_count = lax.axis_size("sp")
    images = level_four.shape[0]
    four, six, cot_four, cot_six = (a[0] for a in (level_four, level_six, cotan_four, cotan_six))
    rows_four, cols_four, chan = four.shape
    rows_six, cols_six = six.shape[:2]
    pitch_four, pitch_six = pitch_of(cols_four), pitch_of(cols_six)
    counts = (
        float(images * GROUP * rows_four * sp_count * cols_four),
        float(images * GROUP * rows_six * sp_count * cols_six),
    )
    found, four = lax.optimization_barrier((places(), four))
    above, below = edges(four, six, cot_four, cot_six)
    vmem = pl.BlockSpec(memory_space=pltpu.VMEM)
    hbm = pl.BlockSpec(memory_space=pltpu.HBM)
    params = pltpu.CompilerParams(vmem_limit_bytes=VMEM_LIMIT)
    framed_four = jax.ShapeDtypeStruct((rows_four + 2, pitch_four, chan), BF16)
    framed_six = jax.ShapeDtypeStruct((rows_six + 2, pitch_six, chan), BF16)
    four_sums = jax.ShapeDtypeStruct((4, chan), F32)
    flops = 2 * 9 * chan * chan * (rows_four * cols_four + rows_six * cols_six)

    def cost(share, size):
        return pl.CostEstimate(flops=int(flops * share), bytes_accessed=size, transcendentals=0)

    inner_four, inner_six, inner_moments = pl.pallas_call(
        inner_kernel,
        out_shape=(
            jax.ShapeDtypeStruct((rows_four - 2, pitch_four, chan), BF16),
            jax.ShapeDtypeStruct((rows_six - 2, pitch_six, chan), BF16),
            four_sums,
        ),
        in_specs=[vmem] * 3,
        out_specs=(vmem, vmem, vmem),
        scratch_shapes=[
            pltpu.VMEM((rows_four, pitch_four, 3 * chan), BF16),
            pltpu.VMEM((rows_six, pitch_six, 3 * chan), BF16),
        ],
        compiler_params=params,
        cost_estimate=cost(1, 4 * four.size),
        name="forward_inner",
    )(four, six, conv_weight)
    outer_four, outer_six, moments = pl.pallas_call(
        functools.partial(outer_kernel, sp_count),
        out_shape=(
            jax.ShapeDtypeStruct((4, pitch_four, chan), BF16),
            jax.ShapeDtypeStruct((4, pitch_six, chan), BF16),
            four_sums,
        ),
        in_specs=[vmem] * 6,
        out_specs=(vmem, vmem, vmem),
        scratch_shapes=[
            pltpu.VMEM((8, pitch_four, 3 * chan), BF16),
            pltpu.VMEM((8, pitch_six, 3 * chan), BF16),
        ],
        compiler_params=params,
        cost_estimate=cost(0.1, four.size),
        name="forward_outer",
    )(four, six, above, below, conv_weight, inner_moments)
    moments, four, six = lax.optimization_barrier((moments, four, six))
    turned_features = pl.pallas_call(
        turn_kernel,
        out_shape=jax.ShapeDtypeStruct((chan, rows_four * cols_four + rows_six * pitch_six), BF16),
        in_specs=[vmem] * 2,
        out_specs=vmem,
        compiler_params=params,
        cost_estimate=cost(0.3, 4 * four.size),
        name="turn",
    )(four, six)
    moments, turned_features = lax.optimization_barrier((group_sum(moments), turned_features))

    slope_four, slope_six, slopes = pl.pallas_call(
        functools.partial(slope_kernel, counts),
        out_shape=(
            jax.ShapeDtypeStruct(framed_four.shape, F32),
            jax.ShapeDtypeStruct(framed_six.shape, F32),
            four_sums,
        ),
        in_specs=[vmem] * 11,
        out_specs=(vmem,) * 3,
        compiler_params=params,
        cost_estimate=cost(0.01, 4 * four.size),
        name="slopes",
    )(
        inner_four, inner_six, outer_four, outer_six, cot_four, cot_six, above, below, moments, bn_gain, bn_shift
    )
    slopes = group_sum(slopes)

    share = chan // sp_count
    wide_four, wide_six = (
        jax.ShapeDtypeStruct(framed.shape[:2] + (3 * chan,), BF16) for framed in (framed_four, framed_six)
    )
    three_four, three_six, own, sent = pl.pallas_call(
        functools.partial(backward_kernel, counts, sp_count, (cols_four, cols_six)),
        out_shape=(
            wide_four,
            wide_six,
            jax.ShapeDtypeStruct((9, share, chan), F32),
            jax.ShapeDtypeStruct((sp_count - 1, 9, share, chan), BF16),
        ),
        in_specs=[vmem] * 11,
        out_specs=(vmem,) * 4,
        scratch_shapes=[pltpu.VMEM((chan, 9 * chan), F32)],
        compiler_params=params,
        cost_estimate=cost(1.2, 8 * four.size),
        name="backward",
    )(
        turned_features, inner_four, inner_six, outer_four, outer_six, slope_four, slope_six, moments, slopes,
        bn_gain, bn_shift,
    )

    piece, pieces = scatter_start(own, sent, found)
    pieces, three_four = lax.optimization_barrier((pieces, three_four))
    met = fours(pieces, 1)
    chunks = chunks_of(rows_four, 8)
    split = -(-2 * len(chunks) // 3)
    done = chunks[split - 1][1]
    grad_first, turned = pl.pallas_call(
        functools.partial(input_first_kernel, chunks[:split]),
        out_shape=(
            jax.ShapeDtypeStruct((done, cols_four, chan), BF16),
            jax.ShapeDtypeStruct((9 * chan, chan), BF16),
        ),
        in_specs=[vmem] * 2,
        out_specs=(vmem, vmem),
        compiler_params=params,
        cost_estimate=cost(0.6, 3 * four.size),
        name="inputs_first",
    )(three_four, conv_weight)
    met, grad_first = lax.optimization_barrier((met, grad_first))

    piece = added(piece, met).astype(BF16)
    piece, three_six = lax.optimization_barrier((piece, three_six))
    met = swap_mixed(piece, RADIX, 2 * RADIX)
    grad_four, grad_six = pl.pallas_call(
        functools.partial(input_second_kernel, chunks[split:], done),
        out_shape=(
            jax.ShapeDtypeStruct(four.shape, BF16),
            jax.ShapeDtypeStruct(six.shape, BF16),
        ),
        in_specs=[vmem] * 4,
        out_specs=(hbm, hbm),
        scratch_shapes=[
            pltpu.VMEM((max(rows_four - done, 1), cols_four, chan), BF16),
            pltpu.VMEM(six.shape, BF16),
            pltpu.SemaphoreType.DMA,
            pltpu.SemaphoreType.DMA((len(chunks),)),
            pltpu.SemaphoreType.DMA((len(chunks_of(rows_six, 12)),)),
        ],
        compiler_params=params,
        cost_estimate=cost(0.4, 2 * four.size),
        name="inputs_second",
    )(three_four, three_six, turned, grad_first)
    met, grad_six = lax.optimization_barrier((met, grad_six))
    piece = both(piece, met)
    piece = both(piece, swap_mixed(piece, 2 * RADIX, RADIX))
    grad_weight = weight_gather(piece, found).reshape(own.shape)
    totals = every_group(slopes)
    grad_gain = jnp.stack([totals[1], totals[3]])
    grad_shift = jnp.stack([totals[0], totals[2]])
    return (grad_four[None], grad_six[None], grad_weight, grad_gain, grad_shift)


def solution(mesh):
    placed = (
        P("rep", "sp", None, None),
        P("rep", "sp", None, None),
        P(),
        P(),
        P(),
        P("rep", "sp", None, None),
        P("rep", "sp", None, None),
    )
    return jax.shard_map(
        local,
        mesh=mesh,
        in_specs=placed,
        out_specs=(
            P("rep", "sp", None, None),
            P("rep", "sp", None, None),
            P(None, "sp", None),
            P(),
            P(),
        ),
        check_vma=False,
    )
```

profile of v0, /device:TPU:0, one launch (start us, length us, event | category | flops | bytes accessed | tf_op | source)
XLA Modules:
  0.0 83.7 jit_solution(15012107243537933895)
XLA Ops:
  0.7 1.7 %edges.1 = bf16[384,256]{1,0:T(8,128)(2,1)} custom-call(bf16[48,96,256]{2,1,0:T(8,128)(2,1)} %bitcast.34, bf16[12,24,256]{2,1,0:T(8,128)(2,1)} %bitcast.42, bf16[48,96,256]{2,1,0:T(8,128)(2,1)} %bitcast.38, bf16[12,24,256]{2,1,0:T(8,128)(2,1)} %bitcast.46), custom_call_target="tpu_custom_call" | custom-call | tf_op jit(solution)/shard_map/edges/pallas_call | solution.py:421
  2.4 0.5 collective-permute-start
  2.9 5.8 %forward_inner.1 = (bf16[46,96,256]{2,1,0:T(8,128)(2,1)S(1)}, bf16[10,32,256]{2,1,0:T(8,128)(2,1)S(1)}, f32[4,256]{1,0:T(4,128)S(1)}) custom-call(bf16[48,96,256]{2,1,0:T(8,128)(2,1)S(1)} %bitcast.35, bf16[12,24,256]{2,1,0:T(8,128)(2,1)S(1)} %bitcast.43, bf16[9,256,256]{2,1,0:T(8,128)(2,1)S(1)} %copy-done.2), custom_call_target="tpu_custom_call" | custom-call | flops 5775556608 | bytes 4718592 | tf_op jit(solution)/shard_map/forward_inner/pallas_call | solution.py:558
  8.8 0.0 collective-permute-done.above_ref.below_ref
  8.8 0.8 forward_outer.1
  9.6 0.4 collective-permute-start.1
  10.0 0.9 %collective-permute-done.1 = f32[4,256]{1,0:T(4,128)S(1)} collective-permute-done((f32[4,256]{1,0:T(4,128)S(1)}, f32[4,256]{1,0:T(4,128)S(1)}, u32[]{:S(2)}, u32[]{:S(2)}) %collective-permute-start.1) | collective-permute-done | bytes 4128 | tf_op jit(solution)/shard_map/ppermute | solution.py:379
  10.8 2.6 %collective-permute-start.3 = (f32[4,256]{1,0:T(4,128)S(1)}, f32[4,256]{1,0:T(4,128)S(1)}, u32[]{:S(2)}, u32[]{:S(2)}) collective-permute-start(f32[4,256]{1,0:T(4,128)S(1)} %add.75), channel_id=1, source_target_pairs={{0,5},{1,4},{2,7},{3,6},{4,1},{5,0},{6,3},{7,2},{8,13},{9,12},{10,... | collective-permute-start | bytes 12296 | tf_op jit(solution)/shard_map/ppermute | solution.py:449
  13.5 1.3 %collective-permute-start.4 = (f32[4,256]{1,0:T(4,128)S(1)}, f32[4,256]{1,0:T(4,128)S(1)}, u32[]{:S(2)}, u32[]{:S(2)}) collective-permute-start(f32[4,256]{1,0:T(4,128)S(1)} %add.75), channel_id=1, source_target_pairs={{0,7},{1,6},{2,5},{3,4},{4,3},{5,2},{6,1},{7,0},{8,15},{9,14},{10,... | collective-permute-start | bytes 12296 | tf_op jit(solution)/shard_map/ppermute | solution.py:449
  14.8 0.1 collective-permute-start.2
  14.9 0.0 collective-permute-done.3
  14.9 2.5 %collective-permute-done.4 = f32[4,256]{1,0:T(4,128)S(1)} collective-permute-done((f32[4,256]{1,0:T(4,128)S(1)}, f32[4,256]{1,0:T(4,128)S(1)}, u32[]{:S(2)}, u32[]{:S(2)}) %collective-permute-start.4) | collective-permute-done | bytes 4128 | tf_op jit(solution)/shard_map/ppermute | solution.py:449
  17.4 0.4 collective-permute-done.2
  17.8 0.0 copy-start.6
  17.9 2.5 %collective-permute-start.6 = (f32[4,256]{1,0:T(4,128)S(1)}, f32[4,256]{1,0:T(4,128)S(1)}, u32[]{:S(2)}, u32[]{:S(2)}) collective-permute-start(f32[4,256]{1,0:T(4,128)S(1)} %add_add_fusion.3), channel_id=1, source_target_pairs={{0,17},{1,16},{2,19},{3,18},{4,21},{5,20},{6,23},{7,22},{8,25},{9,... | collective-permute-start | bytes 12296 | tf_op jit(solution)/shard_map/ppermute | solution.py:449
  20.3 1.3 %collective-permute-start.7 = (f32[4,256]{1,0:T(4,128)S(1)}, f32[4,256]{1,0:T(4,128)S(1)}, u32[]{:S(2)}, u32[]{:S(2)}) collective-permute-start(f32[4,256]{1,0:T(4,128)S(1)} %add_add_fusion.3), channel_id=1, source_target_pairs={{0,25},{1,24},{2,27},{3,26},{4,29},{5,28},{6,31},{7,30},{8,17},{9,... | collective-permute-start | bytes 12296 | tf_op jit(solution)/shard_map/ppermute | solution.py:449
  21.6 0.2 collective-permute-start.5
  21.8 0.7 turn.1.turned_ref
  22.5 0.0 collective-permute-done.6
  22.5 2.6 %collective-permute-done.7 = f32[4,256]{1,0:T(4,128)S(1)} collective-permute-done((f32[4,256]{1,0:T(4,128)S(1)}, f32[4,256]{1,0:T(4,128)S(1)}, u32[]{:S(2)}, u32[]{:S(2)}) %collective-permute-start.7) | collective-permute-done | bytes 4128 | tf_op jit(solution)/shard_map/ppermute | solution.py:449
  25.1 0.0 collective-permute-done.5
  25.2 2.8 %slopes.1 = (f32[50,96,256]{2,1,0:T(8,128)S(1)}, f32[14,32,256]{2,1,0:T(8,128)S(1)}, f32[4,256]{1,0:T(4,128)S(1)}) custom-call(bf16[46,96,256]{2,1,0:T(8,128)(2,1)S(1)} %get-tuple-element.51.inner_four_ref, bf16[10,32,256]{2,1,0:T(8,128)(2,1)S(1)} %get-tuple-element.52.inner_six_ref, bf16[4,96,256]{2,1,0:T(8,128)(2,1)S(1)} %get-tuple-element.53.outer_four_ref, ...), custom_call_target="tpu_custom_call" | custom-call | flops 57755568 | bytes 4718592 | tf_op jit(solution)/shard_map/slopes/pallas_call | solution.py:604
  28.0 0.4 collective-permute-start.8
  28.4 0.9 %collective-permute-done.8 = f32[4,256]{1,0:T(4,128)S(1)} collective-permute-done((f32[4,256]{1,0:T(4,128)S(1)}, f32[4,256]{1,0:T(4,128)S(1)}, u32[]{:S(2)}, u32[]{:S(2)}) %collective-permute-start.8) | collective-permute-done | bytes 4128 | tf_op jit(solution)/shard_map/ppermute | solution.py:379
  29.3 1.4 %collective-permute-start.10 = (f32[4,256]{1,0:T(4,128)S(1)}, f32[4,256]{1,0:T(4,128)S(1)}, u32[]{:S(2)}, u32[]{:S(2)}) collective-permute-start(f32[4,256]{1,0:T(4,128)S(1)} %add.82), channel_id=1, source_target_pairs={{0,5},{1,4},{2,7},{3,6},{4,1},{5,0},{6,3},{7,2},{8,13},{9,12},{10,... | collective-permute-start | bytes 12296 | tf_op jit(solution)/shard_map/ppermute | solution.py:449
  30.7 0.9 %collective-permute-start.11 = (f32[4,256]{1,0:T(4,128)S(1)}, f32[4,256]{1,0:T(4,128)S(1)}, u32[]{:S(2)}, u32[]{:S(2)}) collective-permute-start(f32[4,256]{1,0:T(4,128)S(1)} %add.82), channel_id=1, source_target_pairs={{0,7},{1,6},{2,5},{3,4},{4,3},{5,2},{6,1},{7,0},{8,15},{9,14},{10,... | collective-permute-start | bytes 12296 | tf_op jit(solution)/shard_map/ppermute | solution.py:449
  31.6 0.8 collective-permute-start.9
  32.4 0.0 collective-permute-done.10
  32.4 2.2 %collective-permute-done.11 = f32[4,256]{1,0:T(4,128)S(1)} collective-permute-done((f32[4,256]{1,0:T(4,128)S(1)}, f32[4,256]{1,0:T(4,128)S(1)}, u32[]{:S(2)}, u32[]{:S(2)}) %collective-permute-start.11) | collective-permute-done | bytes 4128 | tf_op jit(solution)/shard_map/ppermute | solution.py:449
  34.6 0.0 collective-permute-done.9
  34.7 1.0 %collective-permute-start.13 = (f32[4,256]{1,0:T(4,128)S(1)}, f32[4,256]{1,0:T(4,128)S(1)}, u32[]{:S(2)}, u32[]{:S(2)}) collective-permute-start(f32[4,256]{1,0:T(4,128)S(1)} %add_add_fusion.1), channel_id=1, source_target_pairs={{0,17},{1,16},{2,19},{3,18},{4,21},{5,20},{6,23},{7,22},{8,25},{9,... | collective-permute-start | bytes 12296 | tf_op jit(solution)/shard_map/ppermute | solution.py:449
  35.7 1.0 %collective-permute-start.14 = (f32[4,256]{1,0:T(4,128)S(1)}, f32[4,256]{1,0:T(4,128)S(1)}, u32[]{:S(2)}, u32[]{:S(2)}) collective-permute-start(f32[4,256]{1,0:T(4,128)S(1)} %add_add_fusion.1), channel_id=1, source_target_pairs={{0,25},{1,24},{2,27},{3,26},{4,29},{5,28},{6,31},{7,30},{8,17},{9,... | collective-permute-start | bytes 12296 | tf_op jit(solution)/shard_map/ppermute | solution.py:449
  36.7 1.1 %collective-permute-start.12 = (f32[4,256]{1,0:T(4,128)S(1)}, f32[4,256]{1,0:T(4,128)S(1)}, u32[]{:S(2)}, u32[]{:S(2)}) collective-permute-start(f32[4,256]{1,0:T(4,128)S(1)} %add_add_fusion.1), channel_id=1, source_target_pairs={{0,9},{1,8},{2,11},{3,10},{4,13},{5,12},{6,15},{7,14},{8,1},{9,0},... | collective-permute-start | bytes 12296 | tf_op jit(solution)/shard_map/ppermute | solution.py:449
  37.7 0.9 %collective-permute-done.13 = f32[4,256]{1,0:T(4,128)S(1)} collective-permute-done((f32[4,256]{1,0:T(4,128)S(1)}, f32[4,256]{1,0:T(4,128)S(1)}, u32[]{:S(2)}, u32[]{:S(2)}) %collective-permute-start.13) | collective-permute-done | bytes 4128 | tf_op jit(solution)/shard_map/ppermute | solution.py:449
  38.7 1.8 %collective-permute-done.14 = f32[4,256]{1,0:T(4,128)S(1)} collective-permute-done((f32[4,256]{1,0:T(4,128)S(1)}, f32[4,256]{1,0:T(4,128)S(1)}, u32[]{:S(2)}, u32[]{:S(2)}) %collective-permute-start.14) | collective-permute-done | bytes 4128 | tf_op jit(solution)/shard_map/ppermute | solution.py:449
  40.5 0.0 collective-permute-done.12
  40.5 7.3 %backward.1 = (bf16[50,96,768]{2,1,0:T(8,128)(2,1)S(1)}, bf16[14,32,768]{2,1,0:T(8,128)(2,1)S(1)}, f32[9,128,256]{2,1,0:T(8,128)S(1)}, bf16[1,9,128,256]{3,2,1,0:T(8,128)(2,1)S(1)}) custom-call(bf16[256,4992]{1,0:T(8,128)(2,1)S(1)} %turn.1.turned_ref, bf16[46,96,256]{2,1,0:T(8,128)(2,1)S(1)} %get-tuple-element.51.inner_four_ref, ...), custom_call_target="tpu_custom_call" | custom-call | flops 6930668032 | bytes 9437184 | tf_op jit(solution)/shard_map/backward/pallas_call | solution.py:625
  47.8 0.3 collective-permute-start.15
  48.1 1.8 %collective-permute-done.15 = bf16[9,128,256]{2,1,0:T(8,128)(2,1)S(1)} collective-permute-done((bf16[9,128,256]{2,1,0:T(8,128)(2,1)S(1)}, bf16[9,128,256]{2,1,0:T(8,128)(2,1)S(1)}, u32[]{:S(2)}, u32[]{:S(2)}) %collective-permute-start.15) | collective-permute-done | bytes 589856 | tf_op jit(solution)/shard_map/ppermute | solution.py:379
  49.9 0.1 fusion.4
  50.0 1.8 %collective-permute-start.16 = (bf16[288,256]{1,0:T(8,128)(2,1)S(1)}, bf16[288,256]{1,0:T(8,128)(2,1)S(1)}, u32[]{:S(2)}, u32[]{:S(2)}) collective-permute-start(bf16[288,256]{1,0:T(8,128)(2,1)S(1)} %get-tuple-element.67), channel_id=1, source_target_pairs={{0,6},{2,4},{4,2},{6,0},{8,14},{10,12},{12,10},{14,8},{16,22},{18,... | collective-permute-start | bytes 442376 | tf_op jit(solution)/shard_map/ppermute | solution.py:379
  51.8 0.5 collective-permute-start.17
  52.3 1.2 %collective-permute-start.18 = (bf16[288,256]{1,0:T(8,128)(2,1)S(1)}, bf16[288,256]{1,0:T(8,128)(2,1)S(1)}, u32[]{:S(2)}, u32[]{:S(2)}) collective-permute-start(bf16[288,256]{1,0:T(8,128)(2,1)S(1)} %get-tuple-element.69), channel_id=1, source_target_pairs={{0,2},{2,0},{4,6},{6,4},{8,10},{10,8},{12,14},{14,12},{16,18},{18,... | collective-permute-start | bytes 442376 | tf_op jit(solution)/shard_map/ppermute | solution.py:379
  53.6 3.9 %inputs_first.1 = (bf16[32,96,256]{2,1,0:T(8,128)(2,1)S(1)}, bf16[2304,256]{1,0:T(8,128)(2,1)S(1)}) custom-call(bf16[50,96,768]{2,1,0:T(8,128)(2,1)S(1)} %get-tuple-element.65.three_four, bf16[9,256,256]{2,1,0:T(8,128)(2,1)S(1)} %copy-done.2), custom_call_target="tpu_custom_call" | custom-call | flops 3465334016 | bytes 3538944 | tf_op jit(solution)/shard_map/inputs_first/pallas_call | solution.py:650
  57.4 0.3 collective-permute-done.16
  57.7 2.4 %collective-permute-done.17 = bf16[288,256]{1,0:T(8,128)(2,1)S(1)} collective-permute-done((bf16[288,256]{1,0:T(8,128)(2,1)S(1)}, bf16[288,256]{1,0:T(8,128)(2,1)S(1)}, u32[]{:S(2)}, u32[]{:S(2)}) %collective-permute-start.17) | collective-permute-done | bytes 147488 | tf_op jit(solution)/shard_map/ppermute | solution.py:379
  60.1 0.0 collective-permute-done.18
  60.1 0.1 fusion.1
  60.2 0.5 collective-permute-start.19
  60.7 3.3 %inputs_second.1 = (bf16[48,96,256]{2,1,0:T(8,128)(2,1)}, bf16[12,24,256]{2,1,0:T(8,128)(2,1)}) custom-call(bf16[50,96,768]{2,1,0:T(8,128)(2,1)S(1)} %get-tuple-element.65.three_four, bf16[14,32,768]{2,1,0:T(8,128)(2,1)S(1)} %get-tuple-element.75.three_six, bf16[2304,256]{1,0:T(8,128)(2,1)S(1)} %get-tuple-element.76.turned, ...), custom_call_target="tpu_custom_call" | custom-call | flops 2310222592 | bytes 2359296 | tf_op jit(solution)/shard_map/inputs_second/pallas_call | solution.py:667
  64.0 3.0 %collective-permute-done.19 = bf16[288,256]{1,0:T(8,128)(2,1)S(1)} collective-permute-done((bf16[288,256]{1,0:T(8,128)(2,1)S(1)}, bf16[288,256]{1,0:T(8,128)(2,1)S(1)}, u32[]{:S(2)}, u32[]{:S(2)}) %collective-permute-start.19) | collective-permute-done | bytes 147488 | tf_op jit(solution)/shard_map/ppermute | solution.py:513
  67.0 0.5 collective-permute-start.20
  67.5 6.8 %collective-permute-done.20 = bf16[288,256]{1,0:T(8,128)(2,1)S(1)} collective-permute-done((bf16[288,256]{1,0:T(8,128)(2,1)S(1)}, bf16[288,256]{1,0:T(8,128)(2,1)S(1)}, u32[]{:S(2)}, u32[]{:S(2)}) %collective-permute-start.20) | collective-permute-done | bytes 147488 | tf_op jit(solution)/shard_map/ppermute | solution.py:513
  74.3 0.1 broadcast_in_dim.15
  74.4 0.1 convert_dynamic-update-slice_fusion.3
  74.5 1.8 %collective-permute-start.21 = (bf16[288,256]{1,0:T(8,128)(2,1)S(1)}, bf16[288,256]{1,0:T(8,128)(2,1)S(1)}, u32[]{:S(2)}, u32[]{:S(2)}) collective-permute-start(bf16[288,256]{1,0:T(8,128)(2,1)S(1)} %get-tuple-element.84), channel_id=1, source_target_pairs={{0,6},{2,4},{4,2},{6,0},{8,14},{10,12},{12,10},{14,8},{16,22},{18,... | collective-permute-start | bytes 442376 | tf_op jit(solution)/shard_map/ppermute | solution.py:379
  76.3 0.6 pad_maximum_fusion
  76.9 0.6 collective-permute-start.22
  77.5 1.2 %collective-permute-start.23 = (bf16[288,256]{1,0:T(8,128)(2,1)S(1)}, bf16[288,256]{1,0:T(8,128)(2,1)S(1)}, u32[]{:S(2)}, u32[]{:S(2)}) collective-permute-start(bf16[288,256]{1,0:T(8,128)(2,1)S(1)} %get-tuple-element.84), channel_id=1, source_target_pairs={{0,2},{2,0},{4,6},{6,4},{8,10},{10,8},{12,14},{14,12},{16,18},{18,... | collective-permute-start | bytes 442376 | tf_op jit(solution)/shard_map/ppermute | solution.py:379
  78.6 2.0 %collective-permute-done.21 = bf16[288,256]{1,0:T(8,128)(2,1)S(1)} collective-permute-done((bf16[288,256]{1,0:T(8,128)(2,1)S(1)}, bf16[288,256]{1,0:T(8,128)(2,1)S(1)}, u32[]{:S(2)}, u32[]{:S(2)}) %collective-permute-start.21) | collective-permute-done | bytes 147488 | tf_op jit(solution)/shard_map/ppermute | solution.py:379
  80.6 1.5 %collective-permute-done.22 = bf16[288,256]{1,0:T(8,128)(2,1)S(1)} collective-permute-done((bf16[288,256]{1,0:T(8,128)(2,1)S(1)}, bf16[288,256]{1,0:T(8,128)(2,1)S(1)}, u32[]{:S(2)}, u32[]{:S(2)}) %collective-permute-start.22) | collective-permute-done | bytes 147488 | tf_op jit(solution)/shard_map/ppermute | solution.py:379
  82.2 0.4 collective-permute-done.23
  82.7 0.0 copy-start.7
  82.7 1.0 %copy-done.7 = f32[4,288,256]{2,1,0:T(8,128)} copy-done((f32[4,288,256]{2,1,0:T(8,128)}, f32[4,288,256]{2,1,0:T(8,128)S(1)}, u32[]{:S(2)}) %copy-start.7) | copy-done | bytes 1179672
  (24 shorter events, 0.2 us)
Async XLA Ops:
  0.6 2.3 %copy-start = (bf16[1,48,96,256]{3,2,1,0:T(8,128)(2,1)S(1)}, bf16[1,48,96,256]{3,2,1,0:T(8,128)(2,1)}, u32[]{:S(2)}) copy-start(bf16[1,48,96,256]{3,2,1,0:T(8,128)(2,1)} %param.7) | copy-start | bytes 7077892
  0.6 2.3 %copy-start.2 = (bf16[9,256,256]{2,1,0:T(8,128)(2,1)S(1)}, bf16[9,256,256]{2,1,0:T(8,128)(2,1)}, u32[]{:S(2)}) copy-start(bf16[9,256,256]{2,1,0:T(8,128)(2,1)} %w_ref.5) | copy-start | bytes 3538948
  0.7 2.3 %copy-start.3 = (bf16[1,12,24,256]{3,2,1,0:T(8,128)(2,1)S(1)}, bf16[1,12,24,256]{3,2,1,0:T(8,128)(2,1)}, u32[]{:S(2)}) copy-start(bf16[1,12,24,256]{3,2,1,0:T(8,128)(2,1)} %param.8) | copy-start | bytes 442372
  2.4 6.4 %collective-permute-start = (bf16[384,256]{1,0:T(8,128)(2,1)}, bf16[384,256]{1,0:T(8,128)(2,1)S(1)}, u32[]{:S(2)}, u32[]{:S(2)}) collective-permute-start(bf16[384,256]{1,0:T(8,128)(2,1)} %edges.1), channel_id=1, source_target_pairs={{0,1},{1,0},{2,3},{3,2},{4,5},{5,4},{6,7},{7,6},{8,9},{9,8},{10,11... | collective-permute-start | bytes 589832 | tf_op jit(solution)/shard_map/ppermute | solution.py:379
  9.6 1.2 %collective-permute-start.1 = (f32[4,256]{1,0:T(4,128)S(1)}, f32[4,256]{1,0:T(4,128)S(1)}, u32[]{:S(2)}, u32[]{:S(2)}) collective-permute-start(f32[4,256]{1,0:T(4,128)S(1)} %get-tuple-element.47), channel_id=1, source_target_pairs={{0,1},{1,0},{2,3},{3,2},{4,5},{5,4},{6,7},{7,6},{8,9},{9,8},{10,11... | collective-permute-start | bytes 12296 | tf_op jit(solution)/shard_map/ppermute | solution.py:379
  10.8 4.0 %collective-permute-start.3 = (f32[4,256]{1,0:T(4,128)S(1)}, f32[4,256]{1,0:T(4,128)S(1)}, u32[]{:S(2)}, u32[]{:S(2)}) collective-permute-start(f32[4,256]{1,0:T(4,128)S(1)} %add.75), channel_id=1, source_target_pairs={{0,5},{1,4},{2,7},{3,6},{4,1},{5,0},{6,3},{7,2},{8,13},{9,12},{10,... | collective-permute-start | bytes 12296 | tf_op jit(solution)/shard_map/ppermute | solution.py:449
  13.5 3.9 %collective-permute-start.4 = (f32[4,256]{1,0:T(4,128)S(1)}, f32[4,256]{1,0:T(4,128)S(1)}, u32[]{:S(2)}, u32[]{:S(2)}) collective-permute-start(f32[4,256]{1,0:T(4,128)S(1)} %add.75), channel_id=1, source_target_pairs={{0,7},{1,6},{2,5},{3,4},{4,3},{5,2},{6,1},{7,0},{8,15},{9,14},{10,... | collective-permute-start | bytes 12296 | tf_op jit(solution)/shard_map/ppermute | solution.py:449
  14.8 3.0 %collective-permute-start.2 = (f32[4,256]{1,0:T(4,128)S(1)}, f32[4,256]{1,0:T(4,128)S(1)}, u32[]{:S(2)}, u32[]{:S(2)}) collective-permute-start(f32[4,256]{1,0:T(4,128)S(1)} %add.75), channel_id=1, source_target_pairs={{0,3},{1,2},{2,1},{3,0},{4,7},{5,6},{6,5},{7,4},{8,11},{9,10},{10,... | collective-permute-start | bytes 12296 | tf_op jit(solution)/shard_map/ppermute | solution.py:449
  17.8 7.3 %copy-start.4 = (bf16[1,12,24,256]{3,2,1,0:T(8,128)(2,1)S(1)}, bf16[1,12,24,256]{3,2,1,0:T(8,128)(2,1)}, u32[]{:S(2)}) copy-start(bf16[1,12,24,256]{3,2,1,0:T(8,128)(2,1)} %param.13) | copy-start | bytes 442372
  17.8 7.3 %copy-start.5 = (f32[2,256]{1,0:T(2,128)S(1)}, f32[2,256]{1,0:T(2,128)}, u32[]{:S(2)}) copy-start(f32[2,256]{1,0:T(2,128)} %gain_ref.3) | copy-start | bytes 6148
  17.8 7.3 %copy-start.6 = (f32[2,256]{1,0:T(2,128)S(1)}, f32[2,256]{1,0:T(2,128)}, u32[]{:S(2)}) copy-start(f32[2,256]{1,0:T(2,128)} %shift_ref.3) | copy-start | bytes 6148
  17.9 4.7 %collective-permute-start.6 = (f32[4,256]{1,0:T(4,128)S(1)}, f32[4,256]{1,0:T(4,128)S(1)}, u32[]{:S(2)}, u32[]{:S(2)}) collective-permute-start(f32[4,256]{1,0:T(4,128)S(1)} %add_add_fusion.3), channel_id=1, source_target_pairs={{0,17},{1,16},{2,19},{3,18},{4,21},{5,20},{6,23},{7,22},{8,25},{9,... | collective-permute-start | bytes 12296 | tf_op jit(solution)/shard_map/ppermute | solution.py:449
  20.3 4.8 %collective-permute-start.7 = (f32[4,256]{1,0:T(4,128)S(1)}, f32[4,256]{1,0:T(4,128)S(1)}, u32[]{:S(2)}, u32[]{:S(2)}) collective-permute-start(f32[4,256]{1,0:T(4,128)S(1)} %add_add_fusion.3), channel_id=1, source_target_pairs={{0,25},{1,24},{2,27},{3,26},{4,29},{5,28},{6,31},{7,30},{8,17},{9,... | collective-permute-start | bytes 12296 | tf_op jit(solution)/shard_map/ppermute | solution.py:449
  21.6 3.6 %collective-permute-start.5 = (f32[4,256]{1,0:T(4,128)S(1)}, f32[4,256]{1,0:T(4,128)S(1)}, u32[]{:S(2)}, u32[]{:S(2)}) collective-permute-start(f32[4,256]{1,0:T(4,128)S(1)} %add_add_fusion.3), channel_id=1, source_target_pairs={{0,9},{1,8},{2,11},{3,10},{4,13},{5,12},{6,15},{7,14},{8,1},{9,0},... | collective-permute-start | bytes 12296 | tf_op jit(solution)/shard_map/ppermute | solution.py:449
  21.8 3.4 %copy-start.1 = (bf16[1,48,96,256]{3,2,1,0:T(8,128)(2,1)S(1)}, bf16[1,48,96,256]{3,2,1,0:T(8,128)(2,1)}, u32[]{:S(2)}) copy-start(bf16[1,48,96,256]{3,2,1,0:T(8,128)(2,1)} %param.12) | copy-start | bytes 7077892
  28.0 1.2 %collective-permute-start.8 = (f32[4,256]{1,0:T(4,128)S(1)}, f32[4,256]{1,0:T(4,128)S(1)}, u32[]{:S(2)}, u32[]{:S(2)}) collective-permute-start(f32[4,256]{1,0:T(4,128)S(1)} %get-tuple-element.58), channel_id=1, source_target_pairs={{0,1},{1,0},{2,3},{3,2},{4,5},{5,4},{6,7},{7,6},{8,9},{9,8},{10,11... | collective-permute-start | bytes 12296 | tf_op jit(solution)/shard_map/ppermute | solution.py:379
  29.3 3.1 %collective-permute-start.10 = (f32[4,256]{1,0:T(4,128)S(1)}, f32[4,256]{1,0:T(4,128)S(1)}, u32[]{:S(2)}, u32[]{:S(2)}) collective-permute-start(f32[4,256]{1,0:T(4,128)S(1)} %add.82), channel_id=1, source_target_pairs={{0,5},{1,4},{2,7},{3,6},{4,1},{5,0},{6,3},{7,2},{8,13},{9,12},{10,... | collective-permute-start | bytes 12296 | tf_op jit(solution)/shard_map/ppermute | solution.py:449
  30.7 3.9 %collective-permute-start.11 = (f32[4,256]{1,0:T(4,128)S(1)}, f32[4,256]{1,0:T(4,128)S(1)}, u32[]{:S(2)}, u32[]{:S(2)}) collective-permute-start(f32[4,256]{1,0:T(4,128)S(1)} %add.82), channel_id=1, source_target_pairs={{0,7},{1,6},{2,5},{3,4},{4,3},{5,2},{6,1},{7,0},{8,15},{9,14},{10,... | collective-permute-start | bytes 12296 | tf_op jit(solution)/shard_map/ppermute | solution.py:449
  31.6 3.0 %collective-permute-start.9 = (f32[4,256]{1,0:T(4,128)S(1)}, f32[4,256]{1,0:T(4,128)S(1)}, u32[]{:S(2)}, u32[]{:S(2)}) collective-permute-start(f32[4,256]{1,0:T(4,128)S(1)} %add.82), channel_id=1, source_target_pairs={{0,3},{1,2},{2,1},{3,0},{4,7},{5,6},{6,5},{7,4},{8,11},{9,10},{10,... | collective-permute-start | bytes 12296 | tf_op jit(solution)/shard_map/ppermute | solution.py:449
  34.7 4.0 %collective-permute-start.13 = (f32[4,256]{1,0:T(4,128)S(1)}, f32[4,256]{1,0:T(4,128)S(1)}, u32[]{:S(2)}, u32[]{:S(2)}) collective-permute-start(f32[4,256]{1,0:T(4,128)S(1)} %add_add_fusion.1), channel_id=1, source_target_pairs={{0,17},{1,16},{2,19},{3,18},{4,21},{5,20},{6,23},{7,22},{8,25},{9,... | collective-permute-start | bytes 12296 | tf_op jit(solution)/shard_map/ppermute | solution.py:449
  35.7 4.8 %collective-permute-start.14 = (f32[4,256]{1,0:T(4,128)S(1)}, f32[4,256]{1,0:T(4,128)S(1)}, u32[]{:S(2)}, u32[]{:S(2)}) collective-permute-start(f32[4,256]{1,0:T(4,128)S(1)} %add_add_fusion.1), channel_id=1, source_target_pairs={{0,25},{1,24},{2,27},{3,26},{4,29},{5,28},{6,31},{7,30},{8,17},{9,... | collective-permute-start | bytes 12296 | tf_op jit(solution)/shard_map/ppermute | solution.py:449
  36.7 3.8 %collective-permute-start.12 = (f32[4,256]{1,0:T(4,128)S(1)}, f32[4,256]{1,0:T(4,128)S(1)}, u32[]{:S(2)}, u32[]{:S(2)}) collective-permute-start(f32[4,256]{1,0:T(4,128)S(1)} %add_add_fusion.1), channel_id=1, source_target_pairs={{0,9},{1,8},{2,11},{3,10},{4,13},{5,12},{6,15},{7,14},{8,1},{9,0},... | collective-permute-start | bytes 12296 | tf_op jit(solution)/shard_map/ppermute | solution.py:449
  47.8 2.1 %collective-permute-start.15 = (bf16[9,128,256]{2,1,0:T(8,128)(2,1)S(1)}, bf16[9,128,256]{2,1,0:T(8,128)(2,1)S(1)}, u32[]{:S(2)}, u32[]{:S(2)}) collective-permute-start(bf16[9,128,256]{2,1,0:T(8,128)(2,1)S(1)} %bitcast.48), channel_id=1, source_target_pairs={{0,1},{1,0},{2,3},{3,2},{4,5},{5,4},{6,7},{7,6},{8,9},{9,8},{10,11... | collective-permute-start | bytes 1769480 | tf_op jit(solution)/shard_map/ppermute | solution.py:379
  50.0 7.7 %collective-permute-start.16 = (bf16[288,256]{1,0:T(8,128)(2,1)S(1)}, bf16[288,256]{1,0:T(8,128)(2,1)S(1)}, u32[]{:S(2)}, u32[]{:S(2)}) collective-permute-start(bf16[288,256]{1,0:T(8,128)(2,1)S(1)} %get-tuple-element.67), channel_id=1, source_target_pairs={{0,6},{2,4},{4,2},{6,0},{8,14},{10,12},{12,10},{14,8},{16,22},{18,... | collective-permute-start | bytes 442376 | tf_op jit(solution)/shard_map/ppermute | solution.py:379
  51.8 8.3 %collective-permute-start.17 = (bf16[288,256]{1,0:T(8,128)(2,1)S(1)}, bf16[288,256]{1,0:T(8,128)(2,1)S(1)}, u32[]{:S(2)}, u32[]{:S(2)}) collective-permute-start(bf16[288,256]{1,0:T(8,128)(2,1)S(1)} %get-tuple-element.68), channel_id=1, source_target_pairs={{0,4},{2,6},{4,0},{6,2},{8,12},{10,14},{12,8},{14,10},{16,20},{18,... | collective-permute-start | bytes 442376 | tf_op jit(solution)/shard_map/ppermute | solution.py:379
  52.3 7.8 %collective-permute-start.18 = (bf16[288,256]{1,0:T(8,128)(2,1)S(1)}, bf16[288,256]{1,0:T(8,128)(2,1)S(1)}, u32[]{:S(2)}, u32[]{:S(2)}) collective-permute-start(bf16[288,256]{1,0:T(8,128)(2,1)S(1)} %get-tuple-element.69), channel_id=1, source_target_pairs={{0,2},{2,0},{4,6},{6,4},{8,10},{10,8},{12,14},{14,12},{16,18},{18,... | collective-permute-start | bytes 442376 | tf_op jit(solution)/shard_map/ppermute | solution.py:379
  60.2 6.8 %collective-permute-start.19 = (bf16[288,256]{1,0:T(8,128)(2,1)S(1)}, bf16[288,256]{1,0:T(8,128)(2,1)S(1)}, u32[]{:S(2)}, u32[]{:S(2)}) collective-permute-start(bf16[288,256]{1,0:T(8,128)(2,1)S(1)} %fusion.1), channel_id=1, source_target_pairs={{0,8},{1,17},{2,10},{3,19},{4,12},{5,21},{6,14},{7,23},{8,0},{9,25... | collective-permute-start | bytes 442376 | tf_op jit(solution)/shard_map/ppermute | solution.py:513
  67.0 7.3 %collective-permute-start.20 = (bf16[288,256]{1,0:T(8,128)(2,1)S(1)}, bf16[288,256]{1,0:T(8,128)(2,1)S(1)}, u32[]{:S(2)}, u32[]{:S(2)}) collective-permute-start(bf16[288,256]{1,0:T(8,128)(2,1)S(1)} %add_convert_fusion.1), channel_id=1, source_target_pairs={{0,16},{1,9},{2,18},{3,11},{4,20},{5,13},{6,22},{7,15},{8,24},{9,1... | collective-permute-start | bytes 442376 | tf_op jit(solution)/shard_map/ppermute | solution.py:513
  74.5 6.1 %collective-permute-start.21 = (bf16[288,256]{1,0:T(8,128)(2,1)S(1)}, bf16[288,256]{1,0:T(8,128)(2,1)S(1)}, u32[]{:S(2)}, u32[]{:S(2)}) collective-permute-start(bf16[288,256]{1,0:T(8,128)(2,1)S(1)} %get-tuple-element.84), channel_id=1, source_target_pairs={{0,6},{2,4},{4,2},{6,0},{8,14},{10,12},{12,10},{14,8},{16,22},{18,... | collective-permute-start | bytes 442376 | tf_op jit(solution)/shard_map/ppermute | solution.py:379
  76.9 5.3 %collective-permute-start.22 = (bf16[288,256]{1,0:T(8,128)(2,1)S(1)}, bf16[288,256]{1,0:T(8,128)(2,1)S(1)}, u32[]{:S(2)}, u32[]{:S(2)}) collective-permute-start(bf16[288,256]{1,0:T(8,128)(2,1)S(1)} %get-tuple-element.84), channel_id=1, source_target_pairs={{0,4},{2,6},{4,0},{6,2},{8,12},{10,14},{12,8},{14,10},{16,20},{18,... | collective-permute-start | bytes 442376 | tf_op jit(solution)/shard_map/ppermute | solution.py:379
  77.5 5.1 %collective-permute-start.23 = (bf16[288,256]{1,0:T(8,128)(2,1)S(1)}, bf16[288,256]{1,0:T(8,128)(2,1)S(1)}, u32[]{:S(2)}, u32[]{:S(2)}) collective-permute-start(bf16[288,256]{1,0:T(8,128)(2,1)S(1)} %get-tuple-element.84), channel_id=1, source_target_pairs={{0,2},{2,0},{4,6},{6,4},{8,10},{10,8},{12,14},{14,12},{16,18},{18,... | collective-permute-start | bytes 442376 | tf_op jit(solution)/shard_map/ppermute | solution.py:379
  82.7 1.0 %copy-start.7 = (f32[4,288,256]{2,1,0:T(8,128)}, f32[4,288,256]{2,1,0:T(8,128)S(1)}, u32[]{:S(2)}) copy-start(f32[4,288,256]{2,1,0:T(8,128)S(1)} %convert_dynamic-update-slice_fusion) | copy-start | bytes 3538948
where the time goes:
time: 83.9 us; the launch traced here: 83.7 us
  waiting for transfers between devices  30.5 us (36%)
  Pallas kernels  26.4 us (31%)
  starting transfers between devices  23.8 us (28%)
  local copies, waits for them, and re-layouts  1.13 us (1%)
  other arithmetic  0.97 us (1%)
  between operations  0.86 us (1%)
    ppermute x12, starting transfers between devices, swap_across(): return lax.ppermute(array, ('rep', 'sp'), pairs)  14.2 us
    ppermute x12, waiting for transfers between devices, swap_across(): return lax.ppermute(array, ('rep', 'sp'), pairs)  10.6 us
    ppermute x10, waiting for transfers between devices, swap(): return lax.ppermute(array, axis, [(i, i ^ stride) for i in range(count)])  10.1 us
    ppermute x2, waiting for transfers between devices, swap_mixed(): return lax.ppermute(array, ('rep', 'sp'), pairs)  9.78 us
    ppermute x10, starting transfers between devices, swap(): return lax.ppermute(array, axis, [(i, i ^ stride) for i in range(count)])  8.67 us
    pallas_call x1, Pallas kernels, local(): pl.pallas_call(functools.partial(backward_kernel, counts, sp_count, (cols...  7.31 us
    pallas_call x1, Pallas kernels, local(): pl.pallas_call(inner_kernel, out_shape=(jax.ShapeDtypeStruct((rows_four -...  5.83 us
    pallas_call x1, Pallas kernels, local(): pl.pallas_call(functools.partial(input_first_kernel, chunks[:split]), out...  3.86 us
  transfers between devices with their start and end apart: 24, of which 16 were waited for; matrix products, arithmetic and copies ran while one was open for 1% of the time, Pallas kernels for 16%

commit v1 on v0

--- a/solution.py
+++ b/solution.py
@@ -24,6 +24,10 @@
 
 def pitch_of(cols):
     return -(-cols // 16) * 16
+
+
+def parity(rep):
+    return ((rep >> 2) ^ (rep >> 3)) & 1
 
 
 def chunks_of(rows, most, multiple=1):
@@ -323,8 +327,9 @@
         dots.append(functools.partial(dot, start, end))
     staged(fills, dots)
     share, chan = own_ref.shape[1:]
+    place = lax.axis_index("sp") ^ parity(lax.axis_index("rep"))
     for step in range(sp_count):
-        begin = pl.multiple_of((lax.axis_index("sp") ^ step) * share, share)
+        begin = pl.multiple_of((place ^ step) * share, share)
         for tap in range(9):
             part = total[pl.ds(begin, share), tap * chan : (tap + 1) * chan]
             if step == 0:
@@ -472,8 +477,9 @@
 
 
 def places():
-    digit = lax.axis_index("rep") & (RADIX - 1)
-    return [digit ^ k for k in range(RADIX)]
+    rep = lax.axis_index("rep")
+    digit = rep & (RADIX - 1)
+    return [digit ^ k for k in range(RADIX)], parity(rep) == 1
 
 
 def piece_of(pieces, index):
@@ -503,10 +509,20 @@
     return [swap(piece, "rep", k * stride) for k, piece in zip(FAR_FIRST, pieces)]
 
 
-def swap_mixed(array, even, odd):
+def swap_high(array, even, odd):
+    count, sp_count = lax.axis_size("rep"), lax.axis_size("sp")
+    pairs = []
+    for rep in range(count):
+        for sp in range(sp_count):
+            stride = odd if (sp ^ parity(rep)) & 1 else even
+            pairs.append((rep * sp_count + sp, (rep ^ stride) * sp_count + (sp ^ 1)))
+    return lax.ppermute(array, ("rep", "sp"), pairs)
+
+
+def bring(array, k):
     count, sp_count = lax.axis_size("rep"), lax.axis_size("sp")
     pairs = [
-        (rep * sp_count + sp, (rep ^ (odd if sp % 2 else even)) * sp_count + sp)
+        (rep * sp_count + sp, (rep ^ k) * sp_count + (sp ^ parity(rep)))
         for rep in range(count)
         for sp in range(sp_count)
     ]
@@ -523,10 +539,11 @@
     while stride < lax.axis_size("rep"):
         total = added(total.astype(F32), fours([total] * 3, stride)).astype(BF16)
         stride = RADIX * stride
-    met = [total] + fours([total] * 3, 1)[::-1]
+    met = {k: bring(total, k) for k in FAR_FIRST}
+    met[0] = jnp.where(found[1], swap(total, "sp", 1), total)
     whole = jnp.zeros((RADIX,) + total.shape, F32)
     for k in (0,) + FAR_FIRST:
-        start = (found[k], 0, 0)
+        start = (found[0][k], 0, 0)
         whole = lax.dynamic_update_slice(whole, met[k][None].astype(F32), start, allow_negative_indices=False)
     return whole
 
@@ -641,7 +658,7 @@
         bn_gain, bn_shift,
     )
 
-    piece, pieces = scatter_start(own, sent, found)
+    piece, pieces = scatter_start(own, sent, found[0])
     pieces, three_four = lax.optimization_barrier((pieces, three_four))
     met = fours(pieces, 1)
     chunks = chunks_of(rows_four, 8)
@@ -659,11 +676,14 @@
         cost_estimate=cost(0.6, 3 * four.size),
         name="inputs_first",
     )(three_four, conv_weight)
-    met, grad_first = lax.optimization_barrier((met, grad_first))
+    totals = every_group(slopes)
+    grad_gain = jnp.stack([totals[1], totals[3]])
+    grad_shift = jnp.stack([totals[0], totals[2]])
+    met, grad_first, grad_gain, grad_shift = lax.optimization_barrier((met, grad_first, grad_gain, grad_shift))
 
     piece = added(piece, met).astype(BF16)
     piece, three_six = lax.optimization_barrier((piece, three_six))
-    met = swap_mixed(piece, RADIX, 2 * RADIX)
+    met = swap_high(piece, RADIX, 2 * RADIX)
     grad_four, grad_six = pl.pallas_call(
         functools.partial(input_second_kernel, chunks[split:], done),
         out_shape=(
@@ -685,11 +705,8 @@
     )(three_four, three_six, turned, grad_first)
     met, grad_six = lax.optimization_barrier((met, grad_six))
     piece = both(piece, met)
-    piece = both(piece, swap_mixed(piece, 2 * RADIX, RADIX))
+    piece = both(piece, swap_high(piece, 2 * RADIX, RADIX))
     grad_weight = weight_gather(piece, found).reshape(own.shape)
-    totals = every_group(slopes)
-    grad_gain = jnp.stack([totals[1], totals[3]])
-    grad_shift = jnp.stack([totals[0], totals[2]])
     return (grad_four[None], grad_six[None], grad_weight, grad_gain, grad_shift)
 
 

time: 83.9 us -> 83.5 us (level)
  waiting for transfers between devices: 30.5 us -> 28.3 us
  starting transfers between devices: 23.8 us -> 25.7 us
    ppermute x10 -> x8, waiting for transfers between devices: 10.1 us -> 5.58 us  [swap(): return lax.ppermute(array, axis, [(i, i ^ stride) for i in range(count)])]
    ppermute x2 -> x5, starting transfers between devices: 1.01 us -> 5.42 us  [the longest x3 3.49 us: bring(): return lax.ppermute(array, ('rep', 'sp'), pairs)]
    ppermute x10 -> x8, starting transfers between devices: 8.67 us -> 6.12 us  [swap(): return lax.ppermute(array, axis, [(i, i ^ stride) for i in range(count)])]
    ppermute x2 -> x5, waiting for transfers between devices: 9.78 us -> 12.1 us  [the longest x3 6.23 us: bring(): return lax.ppermute(array, ('rep', 'sp'), pairs)]
  transfers between devices with their start and end apart: 24 -> 25, of which waited for: 16 -> 15; matrix products, arithmetic and copies ran while one was open for 1% -> 1% of each run, Pallas kernels for 16% -> 16%
where the time goes in v1:
time: 83.5 us; the launch traced here: 83.3 us
  waiting for transfers between devices  28.3 us (34%)
  Pallas kernels  26.3 us (31%)
  starting transfers between devices  25.7 us (31%)
  local copies, waits for them, and re-layouts  1.13 us (1%)
  other arithmetic  1.04 us (1%)
  between operations  0.87 us (1%)
    ppermute x12, starting transfers between devices, swap_across(): return lax.ppermute(array, ('rep', 'sp'), pairs)  14.2 us
    ppermute x12, waiting for transfers between devices, swap_across(): return lax.ppermute(array, ('rep', 'sp'), pairs)  10.6 us
    pallas_call x1, Pallas kernels, local(): pl.pallas_call(functools.partial(backward_kernel, counts, sp_count, (cols...  7.24 us
    ppermute x3, waiting for transfers between devices, bring(): return lax.ppermute(array, ('rep', 'sp'), pairs)  6.23 us
    ppermute x8, starting transfers between devices, swap(): return lax.ppermute(array, axis, [(i, i ^ stride) for i in range(count)])  6.12 us
    ppermute x2, waiting for transfers between devices, swap_high(): return lax.ppermute(array, ('rep', 'sp'), pairs)  5.85 us
    pallas_call x1, Pallas kernels, local(): pl.pallas_call(inner_kernel, out_shape=(jax.ShapeDtypeStruct((rows_four -...  5.83 us
    ppermute x8, waiting for transfers between devices, swap(): return lax.ppermute(array, axis, [(i, i ^ stride) for i in range(count)])  5.58 us
  transfers between devices with their start and end apart: 25, of which 15 were waited for; matrix products, arithmetic and copies ran while one was open for 1% of the time, Pallas kernels for 16%

profile of v1, /device:TPU:0, one launch (start us, length us, event | category | flops | bytes accessed | tf_op | source)
XLA Modules:
  0.0 83.3 jit_solution(12218545477798258197)
XLA Ops:
  0.7 1.7 %edges.1 = bf16[384,256]{1,0:T(8,128)(2,1)} custom-call(bf16[48,96,256]{2,1,0:T(8,128)(2,1)} %bitcast.34, bf16[12,24,256]{2,1,0:T(8,128)(2,1)} %bitcast.42, bf16[48,96,256]{2,1,0:T(8,128)(2,1)} %bitcast.38, bf16[12,24,256]{2,1,0:T(8,128)(2,1)} %bitcast.46), custom_call_target="tpu_custom_call" | custom-call | tf_op jit(solution)/shard_map/edges/pallas_call | solution.py:426
  2.4 0.5 collective-permute-start
  2.9 5.8 %forward_inner.1 = (bf16[46,96,256]{2,1,0:T(8,128)(2,1)S(1)}, bf16[10,32,256]{2,1,0:T(8,128)(2,1)S(1)}, f32[4,256]{1,0:T(4,128)S(1)}) custom-call(bf16[48,96,256]{2,1,0:T(8,128)(2,1)S(1)} %bitcast.35, bf16[12,24,256]{2,1,0:T(8,128)(2,1)S(1)} %bitcast.43, bf16[9,256,256]{2,1,0:T(8,128)(2,1)S(1)} %copy-done.2), custom_call_target="tpu_custom_call" | custom-call | flops 5775556608 | bytes 4718592 | tf_op jit(solution)/shard_map/forward_inner/pallas_call | solution.py:575
  8.8 0.0 collective-permute-done.above_ref.below_ref
  8.8 0.8 forward_outer.1
  9.6 0.4 collective-permute-start.1
  10.0 0.9 %collective-permute-done.1 = f32[4,256]{1,0:T(4,128)S(1)} collective-permute-done((f32[4,256]{1,0:T(4,128)S(1)}, f32[4,256]{1,0:T(4,128)S(1)}, u32[]{:S(2)}, u32[]{:S(2)}) %collective-permute-start.1) | collective-permute-done | bytes 4128 | tf_op jit(solution)/shard_map/ppermute | solution.py:384
  10.8 2.6 %collective-permute-start.3 = (f32[4,256]{1,0:T(4,128)S(1)}, f32[4,256]{1,0:T(4,128)S(1)}, u32[]{:S(2)}, u32[]{:S(2)}) collective-permute-start(f32[4,256]{1,0:T(4,128)S(1)} %add.75), channel_id=1, source_target_pairs={{0,5},{1,4},{2,7},{3,6},{4,1},{5,0},{6,3},{7,2},{8,13},{9,12},{10,... | collective-permute-start | bytes 12296 | tf_op jit(solution)/shard_map/ppermute | solution.py:454
  13.4 1.3 %collective-permute-start.4 = (f32[4,256]{1,0:T(4,128)S(1)}, f32[4,256]{1,0:T(4,128)S(1)}, u32[]{:S(2)}, u32[]{:S(2)}) collective-permute-start(f32[4,256]{1,0:T(4,128)S(1)} %add.75), channel_id=1, source_target_pairs={{0,7},{1,6},{2,5},{3,4},{4,3},{5,2},{6,1},{7,0},{8,15},{9,14},{10,... | collective-permute-start | bytes 12296 | tf_op jit(solution)/shard_map/ppermute | solution.py:454
  14.8 0.1 collective-permute-start.2
  14.9 0.0 collective-permute-done.3
  14.9 2.5 %collective-permute-done.4 = f32[4,256]{1,0:T(4,128)S(1)} collective-permute-done((f32[4,256]{1,0:T(4,128)S(1)}, f32[4,256]{1,0:T(4,128)S(1)}, u32[]{:S(2)}, u32[]{:S(2)}) %collective-permute-start.4) | collective-permute-done | bytes 4128 | tf_op jit(solution)/shard_map/ppermute | solution.py:454
  17.4 0.4 collective-permute-done.2
  17.8 0.0 copy-start.6
  17.9 2.5 %collective-permute-start.6 = (f32[4,256]{1,0:T(4,128)S(1)}, f32[4,256]{1,0:T(4,128)S(1)}, u32[]{:S(2)}, u32[]{:S(2)}) collective-permute-start(f32[4,256]{1,0:T(4,128)S(1)} %add_add_fusion.3), channel_id=1, source_target_pairs={{0,17},{1,16},{2,19},{3,18},{4,21},{5,20},{6,23},{7,22},{8,25},{9,... | collective-permute-start | bytes 12296 | tf_op jit(solution)/shard_map/ppermute | solution.py:454
  20.3 1.3 %collective-permute-start.7 = (f32[4,256]{1,0:T(4,128)S(1)}, f32[4,256]{1,0:T(4,128)S(1)}, u32[]{:S(2)}, u32[]{:S(2)}) collective-permute-start(f32[4,256]{1,0:T(4,128)S(1)} %add_add_fusion.3), channel_id=1, source_target_pairs={{0,25},{1,24},{2,27},{3,26},{4,29},{5,28},{6,31},{7,30},{8,17},{9,... | collective-permute-start | bytes 12296 | tf_op jit(solution)/shard_map/ppermute | solution.py:454
  21.6 0.2 collective-permute-start.5
  21.8 0.7 turn.1.turned_ref
  22.5 0.0 collective-permute-done.6
  22.5 2.6 %collective-permute-done.7 = f32[4,256]{1,0:T(4,128)S(1)} collective-permute-done((f32[4,256]{1,0:T(4,128)S(1)}, f32[4,256]{1,0:T(4,128)S(1)}, u32[]{:S(2)}, u32[]{:S(2)}) %collective-permute-start.7) | collective-permute-done | bytes 4128 | tf_op jit(solution)/shard_map/ppermute | solution.py:454
  25.2 2.8 %slopes.1 = (f32[50,96,256]{2,1,0:T(8,128)S(1)}, f32[14,32,256]{2,1,0:T(8,128)S(1)}, f32[4,256]{1,0:T(4,128)S(1)}) custom-call(bf16[46,96,256]{2,1,0:T(8,128)(2,1)S(1)} %get-tuple-element.54.inner_four_ref, bf16[10,32,256]{2,1,0:T(8,128)(2,1)S(1)} %get-tuple-element.55.inner_six_ref, bf16[4,96,256]{2,1,0:T(8,128)(2,1)S(1)} %get-tuple-element.56.outer_four_ref, ...), custom_call_target="tpu_custom_call" | custom-call | flops 57755568 | bytes 4718592 | tf_op jit(solution)/shard_map/slopes/pallas_call | solution.py:621
  28.0 0.4 collective-permute-start.8
  28.4 0.9 %collective-permute-done.8 = f32[4,256]{1,0:T(4,128)S(1)} collective-permute-done((f32[4,256]{1,0:T(4,128)S(1)}, f32[4,256]{1,0:T(4,128)S(1)}, u32[]{:S(2)}, u32[]{:S(2)}) %collective-permute-start.8) | collective-permute-done | bytes 4128 | tf_op jit(solution)/shard_map/ppermute | solution.py:384
  29.3 1.4 %collective-permute-start.10 = (f32[4,256]{1,0:T(4,128)S(1)}, f32[4,256]{1,0:T(4,128)S(1)}, u32[]{:S(2)}, u32[]{:S(2)}) collective-permute-start(f32[4,256]{1,0:T(4,128)S(1)} %add.82), channel_id=1, source_target_pairs={{0,5},{1,4},{2,7},{3,6},{4,1},{5,0},{6,3},{7,2},{8,13},{9,12},{10,... | collective-permute-start | bytes 12296 | tf_op jit(solution)/shard_map/ppermute | solution.py:454
  30.7 0.9 %collective-permute-start.11 = (f32[4,256]{1,0:T(4,128)S(1)}, f32[4,256]{1,0:T(4,128)S(1)}, u32[]{:S(2)}, u32[]{:S(2)}) collective-permute-start(f32[4,256]{1,0:T(4,128)S(1)} %add.82), channel_id=1, source_target_pairs={{0,7},{1,6},{2,5},{3,4},{4,3},{5,2},{6,1},{7,0},{8,15},{9,14},{10,... | collective-permute-start | bytes 12296 | tf_op jit(solution)/shard_map/ppermute | solution.py:454
  31.6 0.8 collective-permute-start.9
  32.4 0.0 collective-permute-done.10
  32.4 2.2 %collective-permute-done.11 = f32[4,256]{1,0:T(4,128)S(1)} collective-permute-done((f32[4,256]{1,0:T(4,128)S(1)}, f32[4,256]{1,0:T(4,128)S(1)}, u32[]{:S(2)}, u32[]{:S(2)}) %collective-permute-start.11) | collective-permute-done | bytes 4128 | tf_op jit(solution)/shard_map/ppermute | solution.py:454
  34.6 0.0 collective-permute-done.9
  34.7 1.0 %collective-permute-start.13 = (f32[4,256]{1,0:T(4,128)S(1)}, f32[4,256]{1,0:T(4,128)S(1)}, u32[]{:S(2)}, u32[]{:S(2)}) collective-permute-start(f32[4,256]{1,0:T(4,128)S(1)} %add_add_fusion.1), channel_id=1, source_target_pairs={{0,17},{1,16},{2,19},{3,18},{4,21},{5,20},{6,23},{7,22},{8,25},{9,... | collective-permute-start | bytes 12296 | tf_op jit(solution)/shard_map/ppermute | solution.py:454
  35.7 1.0 %collective-permute-start.14 = (f32[4,256]{1,0:T(4,128)S(1)}, f32[4,256]{1,0:T(4,128)S(1)}, u32[]{:S(2)}, u32[]{:S(2)}) collective-permute-start(f32[4,256]{1,0:T(4,128)S(1)} %add_add_fusion.1), channel_id=1, source_target_pairs={{0,25},{1,24},{2,27},{3,26},{4,29},{5,28},{6,31},{7,30},{8,17},{9,... | collective-permute-start | bytes 12296 | tf_op jit(solution)/shard_map/ppermute | solution.py:454
  36.7 1.1 %collective-permute-start.12 = (f32[4,256]{1,0:T(4,128)S(1)}, f32[4,256]{1,0:T(4,128)S(1)}, u32[]{:S(2)}, u32[]{:S(2)}) collective-permute-start(f32[4,256]{1,0:T(4,128)S(1)} %add_add_fusion.1), channel_id=1, source_target_pairs={{0,9},{1,8},{2,11},{3,10},{4,13},{5,12},{6,15},{7,14},{8,1},{9,0},... | collective-permute-start | bytes 12296 | tf_op jit(solution)/shard_map/ppermute | solution.py:454
  37.7 0.9 %collective-permute-done.13 = f32[4,256]{1,0:T(4,128)S(1)} collective-permute-done((f32[4,256]{1,0:T(4,128)S(1)}, f32[4,256]{1,0:T(4,128)S(1)}, u32[]{:S(2)}, u32[]{:S(2)}) %collective-permute-start.13) | collective-permute-done | bytes 4128 | tf_op jit(solution)/shard_map/ppermute | solution.py:454
  38.7 1.8 %collective-permute-done.14 = f32[4,256]{1,0:T(4,128)S(1)} collective-permute-done((f32[4,256]{1,0:T(4,128)S(1)}, f32[4,256]{1,0:T(4,128)S(1)}, u32[]{:S(2)}, u32[]{:S(2)}) %collective-permute-start.14) | collective-permute-done | bytes 4128 | tf_op jit(solution)/shard_map/ppermute | solution.py:454
  40.5 0.0 collective-permute-done.12
  40.5 7.2 %backward.1 = (bf16[50,96,768]{2,1,0:T(8,128)(2,1)S(1)}, bf16[14,32,768]{2,1,0:T(8,128)(2,1)S(1)}, f32[9,128,256]{2,1,0:T(8,128)S(1)}, bf16[1,9,128,256]{3,2,1,0:T(8,128)(2,1)S(1)}) custom-call(bf16[256,4992]{1,0:T(8,128)(2,1)S(1)} %turn.1.turned_ref, bf16[46,96,256]{2,1,0:T(8,128)(2,1)S(1)} %get-tuple-element.54.inner_four_ref, ...), custom_call_target="tpu_custom_call" | custom-call | flops 6930668032 | bytes 9437184 | tf_op jit(solution)/shard_map/backward/pallas_call | solution.py:642
  47.8 0.3 collective-permute-start.15
  48.0 0.6 pad_maximum_fusion
  48.6 1.2 %collective-permute-done.15 = bf16[9,128,256]{2,1,0:T(8,128)(2,1)S(1)} collective-permute-done((bf16[9,128,256]{2,1,0:T(8,128)(2,1)S(1)}, bf16[9,128,256]{2,1,0:T(8,128)(2,1)S(1)}, u32[]{:S(2)}, u32[]{:S(2)}) %collective-permute-start.15) | collective-permute-done | bytes 589856 | tf_op jit(solution)/shard_map/ppermute | solution.py:384
  49.8 0.1 fusion.4
  50.0 1.8 %collective-permute-start.16 = (bf16[288,256]{1,0:T(8,128)(2,1)S(1)}, bf16[288,256]{1,0:T(8,128)(2,1)S(1)}, u32[]{:S(2)}, u32[]{:S(2)}) collective-permute-start(bf16[288,256]{1,0:T(8,128)(2,1)S(1)} %get-tuple-element.70), channel_id=1, source_target_pairs={{0,6},{2,4},{4,2},{6,0},{8,14},{10,12},{12,10},{14,8},{16,22},{18,... | collective-permute-start | bytes 442376 | tf_op jit(solution)/shard_map/ppermute | solution.py:384
  51.8 0.5 collective-permute-start.17
  52.3 1.2 %collective-permute-start.18 = (bf16[288,256]{1,0:T(8,128)(2,1)S(1)}, bf16[288,256]{1,0:T(8,128)(2,1)S(1)}, u32[]{:S(2)}, u32[]{:S(2)}) collective-permute-start(bf16[288,256]{1,0:T(8,128)(2,1)S(1)} %get-tuple-element.72), channel_id=1, source_target_pairs={{0,2},{2,0},{4,6},{6,4},{8,10},{10,8},{12,14},{14,12},{16,18},{18,... | collective-permute-start | bytes 442376 | tf_op jit(solution)/shard_map/ppermute | solution.py:384
  53.5 3.9 %inputs_first.1 = (bf16[32,96,256]{2,1,0:T(8,128)(2,1)S(1)}, bf16[2304,256]{1,0:T(8,128)(2,1)S(1)}) custom-call(bf16[50,96,768]{2,1,0:T(8,128)(2,1)S(1)} %get-tuple-element.68.three_four, bf16[9,256,256]{2,1,0:T(8,128)(2,1)S(1)} %copy-done.2), custom_call_target="tpu_custom_call" | custom-call | flops 3465334016 | bytes 3538944 | tf_op jit(solution)/shard_map/inputs_first/pallas_call | solution.py:667
  57.4 0.3 collective-permute-done.16
  57.6 2.4 %collective-permute-done.17 = bf16[288,256]{1,0:T(8,128)(2,1)S(1)} collective-permute-done((bf16[288,256]{1,0:T(8,128)(2,1)S(1)}, bf16[288,256]{1,0:T(8,128)(2,1)S(1)}, u32[]{:S(2)}, u32[]{:S(2)}) %collective-permute-start.17) | collective-permute-done | bytes 147488 | tf_op jit(solution)/shard_map/ppermute | solution.py:384
  60.0 0.0 collective-permute-done.18
  60.0 0.1 fusion.1
  60.1 0.2 collective-permute-start.19
  60.3 3.3 %inputs_second.1 = (bf16[48,96,256]{2,1,0:T(8,128)(2,1)}, bf16[12,24,256]{2,1,0:T(8,128)(2,1)}) custom-call(bf16[50,96,768]{2,1,0:T(8,128)(2,1)S(1)} %get-tuple-element.68.three_four, bf16[14,32,768]{2,1,0:T(8,128)(2,1)S(1)} %get-tuple-element.78.three_six, bf16[2304,256]{1,0:T(8,128)(2,1)S(1)} %get-tuple-element.79.turned, ...), custom_call_target="tpu_custom_call" | custom-call | flops 2310222592 | bytes 2359296 | tf_op jit(solution)/shard_map/inputs_second/pallas_call | solution.py:687
  63.6 1.7 %collective-permute-done.19 = bf16[288,256]{1,0:T(8,128)(2,1)S(1)} collective-permute-done((bf16[288,256]{1,0:T(8,128)(2,1)S(1)}, bf16[288,256]{1,0:T(8,128)(2,1)S(1)}, u32[]{:S(2)}, u32[]{:S(2)}) %collective-permute-start.19) | collective-permute-done | bytes 147488 | tf_op jit(solution)/shard_map/ppermute | solution.py:519
  65.3 1.8 %collective-permute-start.20 = (bf16[288,256]{1,0:T(8,128)(2,1)S(1)}, bf16[288,256]{1,0:T(8,128)(2,1)S(1)}, u32[]{:S(2)}, u32[]{:S(2)}) collective-permute-start(bf16[288,256]{1,0:T(8,128)(2,1)S(1)} %add_convert_fusion.1), channel_id=1, source_target_pairs={{0,17},{1,8},{2,19},{3,10},{4,21},{5,12},{6,23},{7,14},{8,1},{9,24... | collective-permute-start | bytes 442376 | tf_op jit(solution)/shard_map/ppermute | solution.py:519
  67.1 4.2 %collective-permute-done.20 = bf16[288,256]{1,0:T(8,128)(2,1)S(1)} collective-permute-done((bf16[288,256]{1,0:T(8,128)(2,1)S(1)}, bf16[288,256]{1,0:T(8,128)(2,1)S(1)}, u32[]{:S(2)}, u32[]{:S(2)}) %collective-permute-start.20) | collective-permute-done | bytes 147488 | tf_op jit(solution)/shard_map/ppermute | solution.py:519
  71.3 1.0 %collective-permute-start.21 = (bf16[288,256]{1,0:T(8,128)(2,1)S(1)}, bf16[288,256]{1,0:T(8,128)(2,1)S(1)}, u32[]{:S(2)}, u32[]{:S(2)}) collective-permute-start(bf16[288,256]{1,0:T(8,128)(2,1)S(1)} %add_convert_fusion), channel_id=1, source_target_pairs={{0,1},{1,0},{2,3},{3,2},{4,5},{5,4},{6,7},{7,6},{8,9},{9,8},{10,11... | collective-permute-start | bytes 442376 | tf_op jit(solution)/shard_map/ppermute | solution.py:384
  72.3 1.9 %collective-permute-start.22 = (bf16[288,256]{1,0:T(8,128)(2,1)S(1)}, bf16[288,256]{1,0:T(8,128)(2,1)S(1)}, u32[]{:S(2)}, u32[]{:S(2)}) collective-permute-start(bf16[288,256]{1,0:T(8,128)(2,1)S(1)} %add_convert_fusion), channel_id=1, source_target_pairs={{0,6},{1,7},{2,4},{3,5},{4,2},{5,3},{6,0},{7,1},{8,15},{9,14},{10,... | collective-permute-start | bytes 442376 | tf_op jit(solution)/shard_map/ppermute | solution.py:529
  74.2 0.7 collective-permute-start.23
  74.9 0.9 %collective-permute-start.24 = (bf16[288,256]{1,0:T(8,128)(2,1)S(1)}, bf16[288,256]{1,0:T(8,128)(2,1)S(1)}, u32[]{:S(2)}, u32[]{:S(2)}) collective-permute-start(bf16[288,256]{1,0:T(8,128)(2,1)S(1)} %add_convert_fusion), channel_id=1, source_target_pairs={{0,2},{1,3},{2,0},{3,1},{4,6},{5,7},{6,4},{7,5},{8,11},{9,10},{10,... | collective-permute-start | bytes 442376 | tf_op jit(solution)/shard_map/ppermute | solution.py:529
  75.8 0.0 collective-permute-done.21
  75.8 0.1 broadcast_in_dim.15
  76.0 4.0 %collective-permute-done.22 = bf16[288,256]{1,0:T(8,128)(2,1)S(1)} collective-permute-done((bf16[288,256]{1,0:T(8,128)(2,1)S(1)}, bf16[288,256]{1,0:T(8,128)(2,1)S(1)}, u32[]{:S(2)}, u32[]{:S(2)}) %collective-permute-start.22) | collective-permute-done | bytes 147488 | tf_op jit(solution)/shard_map/ppermute | solution.py:529
  80.0 2.2 %collective-permute-done.23 = bf16[288,256]{1,0:T(8,128)(2,1)S(1)} collective-permute-done((bf16[288,256]{1,0:T(8,128)(2,1)S(1)}, bf16[288,256]{1,0:T(8,128)(2,1)S(1)}, u32[]{:S(2)}, u32[]{:S(2)}) %collective-permute-start.23) | collective-permute-done | bytes 147488 | tf_op jit(solution)/shard_map/ppermute | solution.py:529
  82.3 0.0 collective-permute-done.24
  82.3 0.0 copy-start.7
  82.3 1.0 %copy-done.7 = f32[4,288,256]{2,1,0:T(8,128)} copy-done((f32[4,288,256]{2,1,0:T(8,128)}, f32[4,288,256]{2,1,0:T(8,128)S(1)}, u32[]{:S(2)}) %copy-start.7) | copy-done | bytes 1179672
  (27 shorter events, 0.2 us)
Async XLA Ops:
  0.6 2.3 %copy-start = (bf16[1,48,96,256]{3,2,1,0:T(8,128)(2,1)S(1)}, bf16[1,48,96,256]{3,2,1,0:T(8,128)(2,1)}, u32[]{:S(2)}) copy-start(bf16[1,48,96,256]{3,2,1,0:T(8,128)(2,1)} %param.7) | copy-start | bytes 7077892
  0.6 2.3 %copy-start.2 = (bf16[9,256,256]{2,1,0:T(8,128)(2,1)S(1)}, bf16[9,256,256]{2,1,0:T(8,128)(2,1)}, u32[]{:S(2)}) copy-start(bf16[9,256,256]{2,1,0:T(8,128)(2,1)} %w_ref.5) | copy-start | bytes 3538948
  0.7 2.3 %copy-start.3 = (bf16[1,12,24,256]{3,2,1,0:T(8,128)(2,1)S(1)}, bf16[1,12,24,256]{3,2,1,0:T(8,128)(2,1)}, u32[]{:S(2)}) copy-start(bf16[1,12,24,256]{3,2,1,0:T(8,128)(2,1)} %param.8) | copy-start | bytes 442372
  2.4 6.4 %collective-permute-start = (bf16[384,256]{1,0:T(8,128)(2,1)}, bf16[384,256]{1,0:T(8,128)(2,1)S(1)}, u32[]{:S(2)}, u32[]{:S(2)}) collective-permute-start(bf16[384,256]{1,0:T(8,128)(2,1)} %edges.1), channel_id=1, source_target_pairs={{0,1},{1,0},{2,3},{3,2},{4,5},{5,4},{6,7},{7,6},{8,9},{9,8},{10,11... | collective-permute-start | bytes 589832 | tf_op jit(solution)/shard_map/ppermute | solution.py:384
  9.6 1.2 %collective-permute-start.1 = (f32[4,256]{1,0:T(4,128)S(1)}, f32[4,256]{1,0:T(4,128)S(1)}, u32[]{:S(2)}, u32[]{:S(2)}) collective-permute-start(f32[4,256]{1,0:T(4,128)S(1)} %get-tuple-element.50), channel_id=1, source_target_pairs={{0,1},{1,0},{2,3},{3,2},{4,5},{5,4},{6,7},{7,6},{8,9},{9,8},{10,11... | collective-permute-start | bytes 12296 | tf_op jit(solution)/shard_map/ppermute | solution.py:384
  10.8 4.0 %collective-permute-start.3 = (f32[4,256]{1,0:T(4,128)S(1)}, f32[4,256]{1,0:T(4,128)S(1)}, u32[]{:S(2)}, u32[]{:S(2)}) collective-permute-start(f32[4,256]{1,0:T(4,128)S(1)} %add.75), channel_id=1, source_target_pairs={{0,5},{1,4},{2,7},{3,6},{4,1},{5,0},{6,3},{7,2},{8,13},{9,12},{10,... | collective-permute-start | bytes 12296 | tf_op jit(solution)/shard_map/ppermute | solution.py:454
  13.4 3.9 %collective-permute-start.4 = (f32[4,256]{1,0:T(4,128)S(1)}, f32[4,256]{1,0:T(4,128)S(1)}, u32[]{:S(2)}, u32[]{:S(2)}) collective-permute-start(f32[4,256]{1,0:T(4,128)S(1)} %add.75), channel_id=1, source_target_pairs={{0,7},{1,6},{2,5},{3,4},{4,3},{5,2},{6,1},{7,0},{8,15},{9,14},{10,... | collective-permute-start | bytes 12296 | tf_op jit(solution)/shard_map/ppermute | solution.py:454
  14.8 3.0 %collective-permute-start.2 = (f32[4,256]{1,0:T(4,128)S(1)}, f32[4,256]{1,0:T(4,128)S(1)}, u32[]{:S(2)}, u32[]{:S(2)}) collective-permute-start(f32[4,256]{1,0:T(4,128)S(1)} %add.75), channel_id=1, source_target_pairs={{0,3},{1,2},{2,1},{3,0},{4,7},{5,6},{6,5},{7,4},{8,11},{9,10},{10,... | collective-permute-start | bytes 12296 | tf_op jit(solution)/shard_map/ppermute | solution.py:454
  17.8 7.3 %copy-start.4 = (bf16[1,12,24,256]{3,2,1,0:T(8,128)(2,1)S(1)}, bf16[1,12,24,256]{3,2,1,0:T(8,128)(2,1)}, u32[]{:S(2)}) copy-start(bf16[1,12,24,256]{3,2,1,0:T(8,128)(2,1)} %param.13) | copy-start | bytes 442372
  17.8 7.3 %copy-start.5 = (f32[2,256]{1,0:T(2,128)S(1)}, f32[2,256]{1,0:T(2,128)}, u32[]{:S(2)}) copy-start(f32[2,256]{1,0:T(2,128)} %gain_ref.3) | copy-start | bytes 6148
  17.8 7.3 %copy-start.6 = (f32[2,256]{1,0:T(2,128)S(1)}, f32[2,256]{1,0:T(2,128)}, u32[]{:S(2)}) copy-start(f32[2,256]{1,0:T(2,128)} %shift_ref.3) | copy-start | bytes 6148
  17.9 4.7 %collective-permute-start.6 = (f32[4,256]{1,0:T(4,128)S(1)}, f32[4,256]{1,0:T(4,128)S(1)}, u32[]{:S(2)}, u32[]{:S(2)}) collective-permute-start(f32[4,256]{1,0:T(4,128)S(1)} %add_add_fusion.3), channel_id=1, source_target_pairs={{0,17},{1,16},{2,19},{3,18},{4,21},{5,20},{6,23},{7,22},{8,25},{9,... | collective-permute-start | bytes 12296 | tf_op jit(solution)/shard_map/ppermute | solution.py:454
  20.3 4.8 %collective-permute-start.7 = (f32[4,256]{1,0:T(4,128)S(1)}, f32[4,256]{1,0:T(4,128)S(1)}, u32[]{:S(2)}, u32[]{:S(2)}) collective-permute-start(f32[4,256]{1,0:T(4,128)S(1)} %add_add_fusion.3), channel_id=1, source_target_pairs={{0,25},{1,24},{2,27},{3,26},{4,29},{5,28},{6,31},{7,30},{8,17},{9,... | collective-permute-start | bytes 12296 | tf_op jit(solution)/shard_map/ppermute | solution.py:454
  21.6 3.6 %collective-permute-start.5 = (f32[4,256]{1,0:T(4,128)S(1)}, f32[4,256]{1,0:T(4,128)S(1)}, u32[]{:S(2)}, u32[]{:S(2)}) collective-permute-start(f32[4,256]{1,0:T(4,128)S(1)} %add_add_fusion.3), channel_id=1, source_target_pairs={{0,9},{1,8},{2,11},{3,10},{4,13},{5,12},{6,15},{7,14},{8,1},{9,0},... | collective-permute-start | bytes 12296 | tf_op jit(solution)/shard_map/ppermute | solution.py:454
  21.8 3.4 %copy-start.1 = (bf16[1,48,96,256]{3,2,1,0:T(8,128)(2,1)S(1)}, bf16[1,48,96,256]{3,2,1,0:T(8,128)(2,1)}, u32[]{:S(2)}) copy-start(bf16[1,48,96,256]{3,2,1,0:T(8,128)(2,1)} %param.12) | copy-start | bytes 7077892
  28.0 1.2 %collective-permute-start.8 = (f32[4,256]{1,0:T(4,128)S(1)}, f32[4,256]{1,0:T(4,128)S(1)}, u32[]{:S(2)}, u32[]{:S(2)}) collective-permute-start(f32[4,256]{1,0:T(4,128)S(1)} %get-tuple-element.61), channel_id=1, source_target_pairs={{0,1},{1,0},{2,3},{3,2},{4,5},{5,4},{6,7},{7,6},{8,9},{9,8},{10,11... | collective-permute-start | bytes 12296 | tf_op jit(solution)/shard_map/ppermute | solution.py:384
  29.3 3.1 %collective-permute-start.10 = (f32[4,256]{1,0:T(4,128)S(1)}, f32[4,256]{1,0:T(4,128)S(1)}, u32[]{:S(2)}, u32[]{:S(2)}) collective-permute-start(f32[4,256]{1,0:T(4,128)S(1)} %add.82), channel_id=1, source_target_pairs={{0,5},{1,4},{2,7},{3,6},{4,1},{5,0},{6,3},{7,2},{8,13},{9,12},{10,... | collective-permute-start | bytes 12296 | tf_op jit(solution)/shard_map/ppermute | solution.py:454
  30.7 3.9 %collective-permute-start.11 = (f32[4,256]{1,0:T(4,128)S(1)}, f32[4,256]{1,0:T(4,128)S(1)}, u32[]{:S(2)}, u32[]{:S(2)}) collective-permute-start(f32[4,256]{1,0:T(4,128)S(1)} %add.82), channel_id=1, source_target_pairs={{0,7},{1,6},{2,5},{3,4},{4,3},{5,2},{6,1},{7,0},{8,15},{9,14},{10,... | collective-permute-start | bytes 12296 | tf_op jit(solution)/shard_map/ppermute | solution.py:454
  31.6 3.0 %collective-permute-start.9 = (f32[4,256]{1,0:T(4,128)S(1)}, f32[4,256]{1,0:T(4,128)S(1)}, u32[]{:S(2)}, u32[]{:S(2)}) collective-permute-start(f32[4,256]{1,0:T(4,128)S(1)} %add.82), channel_id=1, source_target_pairs={{0,3},{1,2},{2,1},{3,0},{4,7},{5,6},{6,5},{7,4},{8,11},{9,10},{10,... | collective-permute-start | bytes 12296 | tf_op jit(solution)/shard_map/ppermute | solution.py:454
  34.7 4.0 %collective-permute-start.13 = (f32[4,256]{1,0:T(4,128)S(1)}, f32[4,256]{1,0:T(4,128)S(1)}, u32[]{:S(2)}, u32[]{:S(2)}) collective-permute-start(f32[4,256]{1,0:T(4,128)S(1)} %add_add_fusion.1), channel_id=1, source_target_pairs={{0,17},{1,16},{2,19},{3,18},{4,21},{5,20},{6,23},{7,22},{8,25},{9,... | collective-permute-start | bytes 12296 | tf_op jit(solution)/shard_map/ppermute | solution.py:454
  35.7 4.8 %collective-permute-start.14 = (f32[4,256]{1,0:T(4,128)S(1)}, f32[4,256]{1,0:T(4,128)S(1)}, u32[]{:S(2)}, u32[]{:S(2)}) collective-permute-start(f32[4,256]{1,0:T(4,128)S(1)} %add_add_fusion.1), channel_id=1, source_target_pairs={{0,25},{1,24},{2,27},{3,26},{4,29},{5,28},{6,31},{7,30},{8,17},{9,... | collective-permute-start | bytes 12296 | tf_op jit(solution)/shard_map/ppermute | solution.py:454
  36.7 3.8 %collective-permute-start.12 = (f32[4,256]{1,0:T(4,128)S(1)}, f32[4,256]{1,0:T(4,128)S(1)}, u32[]{:S(2)}, u32[]{:S(2)}) collective-permute-start(f32[4,256]{1,0:T(4,128)S(1)} %add_add_fusion.1), channel_id=1, source_target_pairs={{0,9},{1,8},{2,11},{3,10},{4,13},{5,12},{6,15},{7,14},{8,1},{9,0},... | collective-permute-start | bytes 12296 | tf_op jit(solution)/shard_map/ppermute | solution.py:454
  47.8 2.1 %collective-permute-start.15 = (bf16[9,128,256]{2,1,0:T(8,128)(2,1)S(1)}, bf16[9,128,256]{2,1,0:T(8,128)(2,1)S(1)}, u32[]{:S(2)}, u32[]{:S(2)}) collective-permute-start(bf16[9,128,256]{2,1,0:T(8,128)(2,1)S(1)} %bitcast.48), channel_id=1, source_target_pairs={{0,1},{1,0},{2,3},{3,2},{4,5},{5,4},{6,7},{7,6},{8,9},{9,8},{10,11... | collective-permute-start | bytes 1769480 | tf_op jit(solution)/shard_map/ppermute | solution.py:384
  50.0 7.7 %collective-permute-start.16 = (bf16[288,256]{1,0:T(8,128)(2,1)S(1)}, bf16[288,256]{1,0:T(8,128)(2,1)S(1)}, u32[]{:S(2)}, u32[]{:S(2)}) collective-permute-start(bf16[288,256]{1,0:T(8,128)(2,1)S(1)} %get-tuple-element.70), channel_id=1, source_target_pairs={{0,6},{2,4},{4,2},{6,0},{8,14},{10,12},{12,10},{14,8},{16,22},{18,... | collective-permute-start | bytes 442376 | tf_op jit(solution)/shard_map/ppermute | solution.py:384
  51.8 8.2 %collective-permute-start.17 = (bf16[288,256]{1,0:T(8,128)(2,1)S(1)}, bf16[288,256]{1,0:T(8,128)(2,1)S(1)}, u32[]{:S(2)}, u32[]{:S(2)}) collective-permute-start(bf16[288,256]{1,0:T(8,128)(2,1)S(1)} %get-tuple-element.71), channel_id=1, source_target_pairs={{0,4},{2,6},{4,0},{6,2},{8,12},{10,14},{12,8},{14,10},{16,20},{18,... | collective-permute-start | bytes 442376 | tf_op jit(solution)/shard_map/ppermute | solution.py:384
  52.3 7.7 %collective-permute-start.18 = (bf16[288,256]{1,0:T(8,128)(2,1)S(1)}, bf16[288,256]{1,0:T(8,128)(2,1)S(1)}, u32[]{:S(2)}, u32[]{:S(2)}) collective-permute-start(bf16[288,256]{1,0:T(8,128)(2,1)S(1)} %get-tuple-element.72), channel_id=1, source_target_pairs={{0,2},{2,0},{4,6},{6,4},{8,10},{10,8},{12,14},{14,12},{16,18},{18,... | collective-permute-start | bytes 442376 | tf_op jit(solution)/shard_map/ppermute | solution.py:384
  60.1 5.1 %collective-permute-start.19 = (bf16[288,256]{1,0:T(8,128)(2,1)S(1)}, bf16[288,256]{1,0:T(8,128)(2,1)S(1)}, u32[]{:S(2)}, u32[]{:S(2)}) collective-permute-start(bf16[288,256]{1,0:T(8,128)(2,1)S(1)} %fusion.1), channel_id=1, source_target_pairs={{0,9},{1,16},{2,11},{3,18},{4,13},{5,20},{6,15},{7,22},{8,25},{9,0... | collective-permute-start | bytes 442376 | tf_op jit(solution)/shard_map/ppermute | solution.py:519
  65.3 6.0 %collective-permute-start.20 = (bf16[288,256]{1,0:T(8,128)(2,1)S(1)}, bf16[288,256]{1,0:T(8,128)(2,1)S(1)}, u32[]{:S(2)}, u32[]{:S(2)}) collective-permute-start(bf16[288,256]{1,0:T(8,128)(2,1)S(1)} %add_convert_fusion.1), channel_id=1, source_target_pairs={{0,17},{1,8},{2,19},{3,10},{4,21},{5,12},{6,23},{7,14},{8,1},{9,24... | collective-permute-start | bytes 442376 | tf_op jit(solution)/shard_map/ppermute | solution.py:519
  71.3 4.5 %collective-permute-start.21 = (bf16[288,256]{1,0:T(8,128)(2,1)S(1)}, bf16[288,256]{1,0:T(8,128)(2,1)S(1)}, u32[]{:S(2)}, u32[]{:S(2)}) collective-permute-start(bf16[288,256]{1,0:T(8,128)(2,1)S(1)} %add_convert_fusion), channel_id=1, source_target_pairs={{0,1},{1,0},{2,3},{3,2},{4,5},{5,4},{6,7},{7,6},{8,9},{9,8},{10,11... | collective-permute-start | bytes 442376 | tf_op jit(solution)/shard_map/ppermute | solution.py:384
  72.3 7.6 %collective-permute-start.22 = (bf16[288,256]{1,0:T(8,128)(2,1)S(1)}, bf16[288,256]{1,0:T(8,128)(2,1)S(1)}, u32[]{:S(2)}, u32[]{:S(2)}) collective-permute-start(bf16[288,256]{1,0:T(8,128)(2,1)S(1)} %add_convert_fusion), channel_id=1, source_target_pairs={{0,6},{1,7},{2,4},{3,5},{4,2},{5,3},{6,0},{7,1},{8,15},{9,14},{10,... | collective-permute-start | bytes 442376 | tf_op jit(solution)/shard_map/ppermute | solution.py:529
  74.2 8.0 %collective-permute-start.23 = (bf16[288,256]{1,0:T(8,128)(2,1)S(1)}, bf16[288,256]{1,0:T(8,128)(2,1)S(1)}, u32[]{:S(2)}, u32[]{:S(2)}) collective-permute-start(bf16[288,256]{1,0:T(8,128)(2,1)S(1)} %add_convert_fusion), channel_id=1, source_target_pairs={{0,4},{1,5},{2,6},{3,7},{4,0},{5,1},{6,2},{7,3},{8,13},{9,12},{10,... | collective-permute-start | bytes 442376 | tf_op jit(solution)/shard_map/ppermute | solution.py:529
  74.9 7.3 %collective-permute-start.24 = (bf16[288,256]{1,0:T(8,128)(2,1)S(1)}, bf16[288,256]{1,0:T(8,128)(2,1)S(1)}, u32[]{:S(2)}, u32[]{:S(2)}) collective-permute-start(bf16[288,256]{1,0:T(8,128)(2,1)S(1)} %add_convert_fusion), channel_id=1, source_target_pairs={{0,2},{1,3},{2,0},{3,1},{4,6},{5,7},{6,4},{7,5},{8,11},{9,10},{10,... | collective-permute-start | bytes 442376 | tf_op jit(solution)/shard_map/ppermute | solution.py:529
  82.3 1.0 %copy-start.7 = (f32[4,288,256]{2,1,0:T(8,128)}, f32[4,288,256]{2,1,0:T(8,128)S(1)}, u32[]{:S(2)}) copy-start(f32[4,288,256]{2,1,0:T(8,128)S(1)} %convert_dynamic-update-slice_fusion) | copy-start | bytes 3538948

commit v2 on v1

--- a/solution.py
+++ b/solution.py
@@ -1,4 +1,5 @@
 import functools
+from typing import NamedTuple
 
 import jax
 import jax.numpy as jnp
@@ -10,6 +11,7 @@
 GROUP = 16
 RADIX = 4
 FAR_FIRST = (3, 2, 1)
+FIRST_TAPS = 4
 EPSILON = 1e-05
 F32 = jnp.float32
 BF16 = jnp.bfloat16
@@ -187,7 +189,7 @@
     moments_ref[...] = inner_ref[...] + jnp.concatenate(sums, 0)
 
 
-def turn_kernel(four_ref, six_ref, turned_ref):
+def turn_kernel(four_ref, six_ref, w_ref, turned_ref, turned_w_ref):
     rows_four, cols_four, chan = four_ref.shape
     rows_six, cols_six = six_ref.shape[:2]
     pitch = pitch_of(cols_six)
@@ -197,6 +199,8 @@
     cells = six_ref[...].astype(F32)
     cells = jnp.concatenate([cells, jnp.zeros((rows_six, pitch - cols_six, chan), F32)], 1).astype(BF16)
     turned_ref[:, rows_four * cols_four :] = cells.reshape(rows_six * pitch, chan).T
+    for tap in range(9):
+        turned_w_ref[tap * chan : (tap + 1) * chan] = w_ref[tap].T
 
 
 def slope_level(inner_ref, outer_ref, cotan_ref, above, below, coefs, slope_ref):
@@ -272,10 +276,20 @@
             dconv = dconv * valid[1]
         put_three(three, row, dconv, cols, True)
 
-    def block(start, end):
-        return beside(three, (start + 2, start + 1, start), end - start)
-
-    return fill_row, block
+    return fill_row
+
+
+def taps_beside(three, start, end, taps):
+    pitch, width = three.shape[1:]
+    chan = width // 3
+    parts = []
+    for row_tap in range(3):
+        low, high = max(taps[0] - 3 * row_tap, 0), min(taps[1] - 3 * row_tap, 3)
+        if low < high:
+            first = start + 2 - row_tap
+            rows = three[first : first + end - start, :, low * chan : high * chan]
+            parts.append(rows.reshape((end - start) * pitch, (high - low) * chan))
+    return jnp.concatenate(parts, 1)
 
 
 def backward_bounds(rows):
@@ -285,11 +299,39 @@
     return bounds
 
 
+def weight_dot(turned_ref, three_four, three_six, total, taps, start, end):
+    rows_four, rows_six = three_four.shape[0] - 2, three_six.shape[0] - 2
+    pitch = three_four.shape[1]
+    first, last = start * pitch, end * pitch
+    rhs = taps_beside(three_four, start, end, taps)
+    if end == rows_four:
+        rhs = jnp.concatenate([rhs, taps_beside(three_six, 0, rows_six, taps)], 0)
+        last = turned_ref.shape[1]
+    term = jnp.dot(turned_ref[:, first:last], rhs, preferred_element_type=F32)
+    total[...] = total[...] + term if start else term
+
+
+def put_shares(total, sp_count, own_ref, sent_ref):
+    taps, share, chan = own_ref.shape
+    place = lax.axis_index("sp") ^ parity(lax.axis_index("rep"))
+    for step in range(sp_count):
+        begin = pl.multiple_of((place ^ step) * share, share)
+        for tap in range(taps):
+            part = total[pl.ds(begin, share), tap * chan : (tap + 1) * chan]
+            if step == 0:
+                own_ref[tap] = part
+            else:
+                sent_ref[step - 1, tap] = part.astype(BF16)
+
+
 def backward_kernel(
     counts, sp_count, cols, turned_ref, inner_four_ref, inner_six_ref, outer_four_ref, outer_six_ref,
-    slope_four_ref, slope_six_ref, moments_ref, slopes_ref, gain_ref, shift_ref, three_four, three_six, own_ref, sent_ref, total,
+    slope_four_ref, slope_six_ref, moments_ref, slopes_ref, gain_ref, shift_ref, three_four, three_six, own_ref,
+    sent_ref, grad_gain_ref, grad_shift_ref, total,
 ):
     valid = edges_valid(sp_count)
+    grad_gain_ref[...] = jnp.concatenate([slopes_ref[1:2], slopes_ref[3:4]], 0)
+    grad_shift_ref[...] = jnp.concatenate([slopes_ref[0:1], slopes_ref[2:3]], 0)
     parts = []
     for level, inner_ref, outer_ref, slope_ref, three in (
         (0, inner_four_ref, outer_four_ref, slope_four_ref, three_four),
@@ -303,20 +345,9 @@
                 cols[level], inner_ref, outer_ref, slope_ref, valid, coefs, slopes_ref[pair], counts[level], three
             )
         )
-    (fill_four, block_four), (fill_six, block_six) = parts
+    fill_four, fill_six = parts
     rows_four, rows_six = three_four.shape[0] - 2, three_six.shape[0] - 2
-    pitch = three_four.shape[1]
     bounds = backward_bounds(rows_four)
-
-    def dot(start, end):
-        first, last = start * pitch, end * pitch
-        rhs = block_four(start, end)
-        if end == rows_four:
-            rhs = jnp.concatenate([rhs, block_six(0, rows_six)], 0)
-            last = turned_ref.shape[1]
-        term = jnp.dot(turned_ref[:, first:last], rhs, preferred_element_type=F32)
-        total[...] = total[...] + term if start else term
-
     fills, dots, done = [], [], 0
     for start, end in zip(bounds[:-1], bounds[1:]):
         todo = [functools.partial(fill_four, row) for row in range(done, end + 2)]
@@ -324,18 +355,17 @@
             todo += [functools.partial(fill_six, row) for row in range(rows_six + 2)]
         fills.append(lambda todo=todo: [fill() for fill in todo])
         done = end + 2
-        dots.append(functools.partial(dot, start, end))
+        dots.append(
+            functools.partial(weight_dot, turned_ref, three_four, three_six, total, (0, FIRST_TAPS), start, end)
+        )
     staged(fills, dots)
-    share, chan = own_ref.shape[1:]
-    place = lax.axis_index("sp") ^ parity(lax.axis_index("rep"))
-    for step in range(sp_count):
-        begin = pl.multiple_of((place ^ step) * share, share)
-        for tap in range(9):
-            part = total[pl.ds(begin, share), tap * chan : (tap + 1) * chan]
-            if step == 0:
-                own_ref[tap] = part
-            else:
-                sent_ref[step - 1, tap] = part.astype(BF16)
+    put_shares(total, sp_count, own_ref, sent_ref)
+
+
+def weight_kernel(sp_count, turned_ref, three_four, three_six, own_ref, sent_ref, total):
+    for start, end in chunks_of(three_four.shape[0] - 2, 16, 4):
+        weight_dot(turned_ref, three_four, three_six, total, (FIRST_TAPS, 9), start, end)
+    put_shares(total, sp_count, own_ref, sent_ref)
 
 
 def input_chunks(three, turned, grad, chunks, offset, sent=None):
@@ -350,19 +380,20 @@
             sent(index, start, end)
 
 
-def input_first_kernel(chunks, three_four, w_ref, grad_ref, turned):
-    chan = w_ref.shape[1]
-    for tap in range(9):
-        turned[tap * chan : (tap + 1) * chan] = w_ref[tap].T
-    input_chunks(three_four, turned, grad_ref, chunks, 0)
-
-
-def input_second_kernel(
-    chunks, done, three_four, three_six, turned, first_ref, grad_four_ref, grad_six_ref,
-    grad_four, grad_six, sem_first, sems_four, sems_six,
-):
-    copies = [pltpu.make_async_copy(first_ref, grad_four_ref.at[:done], sem_first)]
-    copies[0].start()
+def input_kernel(chunks, three_four, turned, grad_ref):
+    input_chunks(three_four, turned, grad_ref, chunks, chunks[0][0])
+
+
+def input_last_kernel(chunks, bounds, three_four, three_six, turned, *rest):
+    count = len(bounds) - 1
+    earlier, rest = rest[:count], rest[count:]
+    grad_four_ref, grad_six_ref, grad_four, grad_six, sems, sems_four, sems_six = rest
+    copies = [
+        pltpu.make_async_copy(part, grad_four_ref.at[bounds[index] : bounds[index + 1]], sems.at[index])
+        for index, part in enumerate(earlier)
+    ]
+    for copy in copies:
+        copy.start()
 
     def sender(grad, grad_ref, offset, sems):
         def sent(index, start, end):
@@ -374,6 +405,7 @@
 
     six_chunks = chunks_of(grad_six.shape[0], 12)
     input_chunks(three_six, turned, grad_six, six_chunks, 0, sender(grad_six, grad_six_ref, 0, sems_six))
+    done = bounds[-1]
     input_chunks(three_four, turned, grad_four, chunks, done, sender(grad_four, grad_four_ref, done, sems_four))
     for copy in copies:
         copy.wait()
@@ -476,10 +508,23 @@
     return sums
 
 
+class Places(NamedTuple):
+    digits: list
+    first: list
+    second: list
+    odd: jax.Array
+
+
 def places():
     rep = lax.axis_index("rep")
-    digit = rep & (RADIX - 1)
-    return [digit ^ k for k in range(RADIX)], parity(rep) == 1
+    digits = [(rep & (RADIX - 1)) ^ k for k in range(RADIX)]
+    second = 9 - FIRST_TAPS
+    return Places(
+        digits,
+        [FIRST_TAPS * digit for digit in digits],
+        [RADIX * FIRST_TAPS + second * digit for digit in digits],
+        parity(rep) == 1,
+    )
 
 
 def piece_of(pieces, index):
@@ -487,15 +532,14 @@
     return lax.dynamic_slice(pieces, (index, 0, 0), sizes, allow_negative_indices=False)[0]
 
 
-def scatter_start(own, sent, place):
-    met = [swap(sent[step], "sp", step + 1) for step in range(sent.shape[0])]
+def scatter_pieces(own, met, found):
     chan = own.shape[2]
     parts = [part.reshape(RADIX, -1, chan) for part in [own] + met]
 
     def piece(k):
-        total = piece_of(parts[0], place[k])
+        total = piece_of(parts[0], found.digits[k])
         for part in parts[1:]:
-            total = total + piece_of(part, place[k]).astype(F32)
+            total = total + piece_of(part, found.digits[k]).astype(F32)
         return total
 
     return piece(0), [piece(k).astype(BF16) for k in FAR_FIRST]
@@ -533,18 +577,23 @@
     return (own.astype(F32) + met.astype(F32)).astype(BF16)
 
 
-def weight_gather(total, found):
-    chan = total.shape[1]
+def every_share(total):
     stride = GROUP
     while stride < lax.axis_size("rep"):
         total = added(total.astype(F32), fours([total] * 3, stride)).astype(BF16)
         stride = RADIX * stride
-    met = {k: bring(total, k) for k in FAR_FIRST}
-    met[0] = jnp.where(found[1], swap(total, "sp", 1), total)
-    whole = jnp.zeros((RADIX,) + total.shape, F32)
-    for k in (0,) + FAR_FIRST:
-        start = (found[0][k], 0, 0)
-        whole = lax.dynamic_update_slice(whole, met[k][None].astype(F32), start, allow_negative_indices=False)
+    return total
+
+
+def gather(total, found):
+    beside = swap(total, "sp", 1)
+    return [bring(total, k) for k in FAR_FIRST] + [jnp.where(found.odd, beside, total)], beside
+
+
+def put_pieces(whole, pieces, starts):
+    for k, piece in zip(FAR_FIRST + (0,), pieces):
+        piece = piece.reshape((-1,) + whole.shape[1:]).astype(F32)
+        whole = lax.dynamic_update_slice(whole, piece, (starts[k], 0, 0), allow_negative_indices=False)
     return whole
 
 
@@ -607,16 +656,19 @@
         name="forward_outer",
     )(four, six, above, below, conv_weight, inner_moments)
     moments, four, six = lax.optimization_barrier((moments, four, six))
-    turned_features = pl.pallas_call(
+    turned, turned_weight = pl.pallas_call(
         turn_kernel,
-        out_shape=jax.ShapeDtypeStruct((chan, rows_four * cols_four + rows_six * pitch_six), BF16),
-        in_specs=[vmem] * 2,
-        out_specs=vmem,
+        out_shape=(
+            jax.ShapeDtypeStruct((chan, rows_four * cols_four + rows_six * pitch_six), BF16),
+            jax.ShapeDtypeStruct((9 * chan, chan), BF16),
+        ),
+        in_specs=[vmem] * 3,
+        out_specs=(vmem, vmem),
         compiler_params=params,
         cost_estimate=cost(0.3, 4 * four.size),
         name="turn",
-    )(four, six)
-    moments, turned_features = lax.optimization_barrier((group_sum(moments), turned_features))
+    )(four, six, conv_weight)
+    moments, turned, turned_weight = lax.optimization_barrier((group_sum(moments), turned, turned_weight))
 
     slope_four, slope_six, slopes = pl.pallas_call(
         functools.partial(slope_kernel, counts),
@@ -639,74 +691,114 @@
     wide_four, wide_six = (
         jax.ShapeDtypeStruct(framed.shape[:2] + (3 * chan,), BF16) for framed in (framed_four, framed_six)
     )
-    three_four, three_six, own, sent = pl.pallas_call(
+    def shares(taps):
+        return (
+            jax.ShapeDtypeStruct((taps, share, chan), F32),
+            jax.ShapeDtypeStruct((sp_count - 1, taps, share, chan), BF16),
+        )
+
+    three_four, three_six, own_a, sent_a, grad_gain, grad_shift = pl.pallas_call(
         functools.partial(backward_kernel, counts, sp_count, (cols_four, cols_six)),
-        out_shape=(
-            wide_four,
-            wide_six,
-            jax.ShapeDtypeStruct((9, share, chan), F32),
-            jax.ShapeDtypeStruct((sp_count - 1, 9, share, chan), BF16),
-        ),
+        out_shape=(wide_four, wide_six) + shares(FIRST_TAPS) + (jax.ShapeDtypeStruct((2, chan), F32),) * 2,
         in_specs=[vmem] * 11,
-        out_specs=(vmem,) * 4,
-        scratch_shapes=[pltpu.VMEM((chan, 9 * chan), F32)],
+        out_specs=(vmem,) * 6,
+        scratch_shapes=[pltpu.VMEM((chan, FIRST_TAPS * chan), F32)],
         compiler_params=params,
-        cost_estimate=cost(1.2, 8 * four.size),
+        cost_estimate=cost(0.6, 8 * four.size),
         name="backward",
     )(
-        turned_features, inner_four, inner_six, outer_four, outer_six, slope_four, slope_six, moments, slopes,
+        turned, inner_four, inner_six, outer_four, outer_six, slope_four, slope_six, moments, slopes,
         bn_gain, bn_shift,
     )
-
-    piece, pieces = scatter_start(own, sent, found[0])
-    pieces, three_four = lax.optimization_barrier((pieces, three_four))
-    met = fours(pieces, 1)
+    sent_a, three_six = lax.optimization_barrier((sent_a, three_six))
+    met_a = [swap(sent_a[step], "sp", step + 1) for step in range(sp_count - 1)]
+    own_b, sent_b = pl.pallas_call(
+        functools.partial(weight_kernel, sp_count),
+        out_shape=shares(9 - FIRST_TAPS),
+        in_specs=[vmem] * 3,
+        out_specs=(vmem, vmem),
+        scratch_shapes=[pltpu.VMEM((chan, (9 - FIRST_TAPS) * chan), F32)],
+        compiler_params=params,
+        cost_estimate=cost(0.6, 8 * four.size),
+        name="weights",
+    )(turned, three_four, three_six)
+    met_a, sent_b = lax.optimization_barrier((met_a, sent_b))
+    met_b = [swap(sent_b[step], "sp", step + 1) for step in range(sp_count - 1)]
+
     chunks = chunks_of(rows_four, 8)
-    split = -(-2 * len(chunks) // 3)
-    done = chunks[split - 1][1]
-    grad_first, turned = pl.pallas_call(
-        functools.partial(input_first_kernel, chunks[:split]),
-        out_shape=(
-            jax.ShapeDtypeStruct((done, cols_four, chan), BF16),
-            jax.ShapeDtypeStruct((9 * chan, chan), BF16),
-        ),
-        in_specs=[vmem] * 2,
-        out_specs=(vmem, vmem),
-        compiler_params=params,
-        cost_estimate=cost(0.6, 3 * four.size),
-        name="inputs_first",
-    )(three_four, conv_weight)
-    totals = every_group(slopes)
-    grad_gain = jnp.stack([totals[1], totals[3]])
-    grad_shift = jnp.stack([totals[0], totals[2]])
-    met, grad_first, grad_gain, grad_shift = lax.optimization_barrier((met, grad_first, grad_gain, grad_shift))
-
-    piece = added(piece, met).astype(BF16)
-    piece, three_six = lax.optimization_barrier((piece, three_six))
-    met = swap_high(piece, RADIX, 2 * RADIX)
+    cuts = [part * len(chunks) // 3 for part in range(4)]
+    groups = [chunks[low:high] for low, high in zip(cuts[:-1], cuts[1:]) if low < high]
+    bounds = [group[0][0] for group in groups]
+
+    def inputs(group, three):
+        return pl.pallas_call(
+            functools.partial(input_kernel, group),
+            out_shape=jax.ShapeDtypeStruct((group[-1][1] - group[0][0], cols_four, chan), BF16),
+            in_specs=[vmem] * 2,
+            out_specs=vmem,
+            compiler_params=params,
+            cost_estimate=cost(0.3, four.size),
+            name="inputs",
+        )(three, turned_weight)
+
+    grad_gain, grad_shift = every_group(grad_gain), every_group(grad_shift)
+
+    piece_a, pieces_a = scatter_pieces(own_a, met_a, found)
+    met_a = fours(pieces_a, 1)
+    piece_b, pieces_b = scatter_pieces(own_b, met_b, found)
+    met_b = fours(pieces_b, 1)
+    met_a, unused = lax.optimization_barrier((met_a, pieces_b))
+
+    piece_a = added(piece_a, met_a).astype(BF16)
+    piece_a, three_four = lax.optimization_barrier((piece_a, three_four))
+    met_a = swap_high(piece_a, RADIX, 2 * RADIX)
+    earlier = [inputs(groups[0], three_four)] if len(groups) > 1 else []
+    met_b, earlier = lax.optimization_barrier((met_b, earlier))
+
+    piece_b = added(piece_b, met_b).astype(BF16)
+    met_b = swap_high(piece_b, RADIX, 2 * RADIX)
+    met_a, unused = lax.optimization_barrier((met_a, piece_b))
+
+    piece_a = both(piece_a, met_a)
+    piece_a, three_four = lax.optimization_barrier((piece_a, three_four))
+    met_a = swap_high(piece_a, 2 * RADIX, RADIX)
+    if len(groups) > 2:
+        earlier = earlier + [inputs(groups[1], three_four)]
+    met_b, earlier = lax.optimization_barrier((met_b, earlier))
+
+    piece_b = both(piece_b, met_b)
+    met_b = swap_high(piece_b, 2 * RADIX, RADIX)
+    met_a, unused = lax.optimization_barrier((met_a, piece_b))
+
+    pieces_a, unused = gather(every_share(both(piece_a, met_a)), found)
+    piece_b = every_share(both(piece_b, met_b))
+    pieces_b, beside = gather(piece_b, found)
+    unused, three_four = lax.optimization_barrier((beside, three_four))
+    done = bounds[-1]
     grad_four, grad_six = pl.pallas_call(
-        functools.partial(input_second_kernel, chunks[split:], done),
+        functools.partial(input_last_kernel, groups[-1], bounds),
         out_shape=(
             jax.ShapeDtypeStruct(four.shape, BF16),
             jax.ShapeDtypeStruct(six.shape, BF16),
         ),
-        in_specs=[vmem] * 4,
+        in_specs=[vmem] * (3 + len(earlier)),
         out_specs=(hbm, hbm),
         scratch_shapes=[
-            pltpu.VMEM((max(rows_four - done, 1), cols_four, chan), BF16),
+            pltpu.VMEM((rows_four - done, cols_four, chan), BF16),
             pltpu.VMEM(six.shape, BF16),
-            pltpu.SemaphoreType.DMA,
+            pltpu.SemaphoreType.DMA((len(groups),)),
             pltpu.SemaphoreType.DMA((len(chunks),)),
             pltpu.SemaphoreType.DMA((len(chunks_of(rows_six, 12)),)),
         ],
         compiler_params=params,
         cost_estimate=cost(0.4, 2 * four.size),
-        name="inputs_second",
-    )(three_four, three_six, turned, grad_first)
-    met, grad_six = lax.optimization_barrier((met, grad_six))
-    piece = both(piece, met)
-    piece = both(piece, swap_high(piece, 2 * RADIX, RADIX))
-    grad_weight = weight_gather(piece, found).reshape(own.shape)
+        name="inputs_last",
+    )(three_four, three_six, turned_weight, *earlier)
+    pieces_a, pieces_b, grad_six = lax.optimization_barrier((pieces_a, pieces_b, grad_six))
+    whole = jnp.zeros((9 * RADIX, share // RADIX, chan), F32)
+    whole = put_pieces(whole, pieces_a, found.first)
+    whole = put_pieces(whole, pieces_b, found.second)
+    grad_weight = whole.reshape(9, share, chan)
     return (grad_four[None], grad_six[None], grad_weight, grad_gain, grad_shift)
 
 

time: 83.5 us -> 81.5 us (0.976)
  waiting for transfers between devices: 28.3 us -> 15.7 us
  starting transfers between devices: 25.7 us -> 35.8 us
    ppermute x3 -> x6, waiting for transfers between devices: 6.23 us -> 0.59 us  [bring(): return lax.ppermute(array, ('rep', 'sp'), pairs)]
    ppermute x2 -> x4, waiting for transfers between devices: 5.85 us -> 0.44 us  [swap_high(): return lax.ppermute(array, ('rep', 'sp'), pairs)]
    pallas_call x3 -> x5, Pallas kernels: 7.84 us -> 11.9 us  [the longest x2 3.97 us: inputs(): pl.pallas_call(functools.partial(input_kernel, group), out_shape=jax.Shap...]
    ppermute x3 -> x6, starting transfers between devices: 3.49 us -> 7.17 us  [bring(): return lax.ppermute(array, ('rep', 'sp'), pairs)]
    pallas_call x1, Pallas kernels: 7.24 us -> 4 us  [local(): pl.pallas_call(functools.partial(backward_kernel, counts, sp_count, (cols...]
    ppermute x8 -> x13, starting transfers between devices: 6.12 us -> 9 us  [swap(): return lax.ppermute(array, axis, [(i, i ^ stride) for i in range(count)])]
    ppermute x2 -> x4, starting transfers between devices: 1.93 us -> 4.7 us  [swap_high(): return lax.ppermute(array, ('rep', 'sp'), pairs)]
    ppermute x8 -> x13, waiting for transfers between devices: 5.58 us -> 3.61 us  [swap(): return lax.ppermute(array, axis, [(i, i ^ stride) for i in range(count)])]
  transfers between devices with their start and end apart: 25 -> 35, of which waited for: 15 -> 15; matrix products, arithmetic and copies ran while one was open for 1% -> 0% of each run, Pallas kernels for 16% -> 22%
where the time goes in v2:
time: 81.5 us; the launch traced here: 81.3 us
  starting transfers between devices  35.8 us (44%)
  Pallas kernels  27.1 us (33%)
  waiting for transfers between devices  15.7 us (19%)
  local copies, waits for them, and re-layouts  1.16 us (1%)
  between operations  1.04 us (1%)
    ppermute x12, starting transfers between devices, swap_across(): return lax.ppermute(array, ('rep', 'sp'), pairs)  14.9 us
    ppermute x12, waiting for transfers between devices, swap_across(): return lax.ppermute(array, ('rep', 'sp'), pairs)  11.1 us
    ppermute x13, starting transfers between devices, swap(): return lax.ppermute(array, axis, [(i, i ^ stride) for i in range(count)])  9 us
    ppermute x6, starting transfers between devices, bring(): return lax.ppermute(array, ('rep', 'sp'), pairs)  7.17 us
    pallas_call x1, Pallas kernels, local(): pl.pallas_call(inner_kernel, out_shape=(jax.ShapeDtypeStruct((rows_four -...  5.83 us
    ppermute x4, starting transfers between devices, swap_high(): return lax.ppermute(array, ('rep', 'sp'), pairs)  4.7 us
    pallas_call x1, Pallas kernels, local(): pl.pallas_call(functools.partial(backward_kernel, counts, sp_count, (cols...  4 us
    pallas_call x2, Pallas kernels, inputs(): pl.pallas_call(functools.partial(input_kernel, group), out_shape=jax.Shap...  3.97 us
  transfers between devices with their start and end apart: 35, of which 15 were waited for; matrix products, arithmetic and copies ran while one was open for 0% of the time, Pallas kernels for 22%

profile of v2, /device:TPU:0, one launch (start us, length us, event | category | flops | bytes accessed | tf_op | source)
XLA Modules:
  0.0 81.3 jit_solution(17355711180657207045)
XLA Ops:
  0.7 1.7 %edges.1 = bf16[384,256]{1,0:T(8,128)(2,1)} custom-call(bf16[48,96,256]{2,1,0:T(8,128)(2,1)} %bitcast.51, bf16[12,24,256]{2,1,0:T(8,128)(2,1)} %bitcast.59, bf16[48,96,256]{2,1,0:T(8,128)(2,1)} %bitcast.55, bf16[12,24,256]{2,1,0:T(8,128)(2,1)} %bitcast.63), custom_call_target="tpu_custom_call" | custom-call | tf_op jit(solution)/shard_map/edges/pallas_call | solution.py:458
  2.4 0.5 collective-permute-start
  3.0 5.8 %forward_inner.1 = (bf16[46,96,256]{2,1,0:T(8,128)(2,1)S(1)}, bf16[10,32,256]{2,1,0:T(8,128)(2,1)S(1)}, f32[4,256]{1,0:T(4,128)S(1)}) custom-call(bf16[48,96,256]{2,1,0:T(8,128)(2,1)S(1)} %bitcast.52, bf16[12,24,256]{2,1,0:T(8,128)(2,1)S(1)} %bitcast.60, bf16[9,256,256]{2,1,0:T(8,128)(2,1)S(1)} %copy-done.2), custom_call_target="tpu_custom_call" | custom-call | flops 5775556608 | bytes 4718592 | tf_op jit(solution)/shard_map/forward_inner/pallas_call | solution.py:624
  8.8 0.8 forward_outer.1
  9.6 0.4 collective-permute-start.1
  10.0 0.9 %collective-permute-done.1 = f32[4,256]{1,0:T(4,128)S(1)} collective-permute-done((f32[4,256]{1,0:T(4,128)S(1)}, f32[4,256]{1,0:T(4,128)S(1)}, u32[]{:S(2)}, u32[]{:S(2)}) %collective-permute-start.1) | collective-permute-done | bytes 4128 | tf_op jit(solution)/shard_map/ppermute | solution.py:416
  10.8 2.6 %collective-permute-start.2 = (f32[4,256]{1,0:T(4,128)S(1)}, f32[4,256]{1,0:T(4,128)S(1)}, u32[]{:S(2)}, u32[]{:S(2)}) collective-permute-start(f32[4,256]{1,0:T(4,128)S(1)} %add.124), channel_id=1, source_target_pairs={{0,3},{1,2},{2,1},{3,0},{4,7},{5,6},{6,5},{7,4},{8,11},{9,10},{10,... | collective-permute-start | bytes 12296 | tf_op jit(solution)/shard_map/ppermute | solution.py:486
  13.4 1.4 %collective-permute-start.3 = (f32[4,256]{1,0:T(4,128)S(1)}, f32[4,256]{1,0:T(4,128)S(1)}, u32[]{:S(2)}, u32[]{:S(2)}) collective-permute-start(f32[4,256]{1,0:T(4,128)S(1)} %add.124), channel_id=1, source_target_pairs={{0,5},{1,4},{2,7},{3,6},{4,1},{5,0},{6,3},{7,2},{8,13},{9,12},{10,... | collective-permute-start | bytes 12296 | tf_op jit(solution)/shard_map/ppermute | solution.py:486
  14.9 1.6 %collective-permute-done.3 = f32[4,256]{1,0:T(4,128)S(1)} collective-permute-done((f32[4,256]{1,0:T(4,128)S(1)}, f32[4,256]{1,0:T(4,128)S(1)}, u32[]{:S(2)}, u32[]{:S(2)}) %collective-permute-start.3) | collective-permute-done | bytes 4128 | tf_op jit(solution)/shard_map/ppermute | solution.py:486
  16.5 2.3 %collective-permute-done.4 = f32[4,256]{1,0:T(4,128)S(1)} collective-permute-done((f32[4,256]{1,0:T(4,128)S(1)}, f32[4,256]{1,0:T(4,128)S(1)}, u32[]{:S(2)}, u32[]{:S(2)}) %collective-permute-start.4) | collective-permute-done | bytes 4128 | tf_op jit(solution)/shard_map/ppermute | solution.py:486
  18.8 0.0 copy-start.6
  18.8 1.5 %collective-permute-start.5 = (f32[4,256]{1,0:T(4,128)S(1)}, f32[4,256]{1,0:T(4,128)S(1)}, u32[]{:S(2)}, u32[]{:S(2)}) collective-permute-start(f32[4,256]{1,0:T(4,128)S(1)} %add_add_fusion.3), channel_id=1, source_target_pairs={{0,9},{1,8},{2,11},{3,10},{4,13},{5,12},{6,15},{7,14},{8,1},{9,0},... | collective-permute-start | bytes 12296 | tf_op jit(solution)/shard_map/ppermute | solution.py:486
  20.3 2.5 %collective-permute-start.6 = (f32[4,256]{1,0:T(4,128)S(1)}, f32[4,256]{1,0:T(4,128)S(1)}, u32[]{:S(2)}, u32[]{:S(2)}) collective-permute-start(f32[4,256]{1,0:T(4,128)S(1)} %add_add_fusion.3), channel_id=1, source_target_pairs={{0,17},{1,16},{2,19},{3,18},{4,21},{5,20},{6,23},{7,22},{8,25},{9,... | collective-permute-start | bytes 12296 | tf_op jit(solution)/shard_map/ppermute | solution.py:486
  22.8 0.0 collective-permute-start.7
  22.8 1.0 %turn.1 = (bf16[256,4992]{1,0:T(8,128)(2,1)S(1)}, bf16[2304,256]{1,0:T(8,128)(2,1)S(1)}) custom-call(bf16[48,96,256]{2,1,0:T(8,128)(2,1)S(1)} %bitcast.54, bf16[12,24,256]{2,1,0:T(8,128)(2,1)S(1)} %bitcast.62, bf16[9,256,256]{2,1,0:T(8,128)(2,1)S(1)} %copy-done.2), custom_call_target="tpu_custom_call" | custom-call | flops 1732667008 | bytes 4718592 | tf_op jit(solution)/shard_map/turn/pallas_call | solution.py:659
  23.8 0.4 collective-permute-done.6
  24.2 3.4 %collective-permute-done.7 = f32[4,256]{1,0:T(4,128)S(1)} collective-permute-done((f32[4,256]{1,0:T(4,128)S(1)}, f32[4,256]{1,0:T(4,128)S(1)}, u32[]{:S(2)}, u32[]{:S(2)}) %collective-permute-start.7) | collective-permute-done | bytes 4128 | tf_op jit(solution)/shard_map/ppermute | solution.py:486
  27.6 2.8 %slopes.1 = (f32[50,96,256]{2,1,0:T(8,128)S(1)}, f32[14,32,256]{2,1,0:T(8,128)S(1)}, f32[4,256]{1,0:T(4,128)S(1)}) custom-call(bf16[46,96,256]{2,1,0:T(8,128)(2,1)S(1)} %get-tuple-element.85.inner_four_ref, bf16[10,32,256]{2,1,0:T(8,128)(2,1)S(1)} %get-tuple-element.86.inner_six_ref, bf16[4,96,256]{2,1,0:T(8,128)(2,1)S(1)} %get-tuple-element.87.outer_four_ref, ...), custom_call_target="tpu_custom_call" | custom-call | flops 57755568 | bytes 4718592 | tf_op jit(solution)/shard_map/slopes/pallas_call | solution.py:673
  30.5 0.3 collective-permute-start.8
  30.8 1.0 %collective-permute-done.8 = f32[4,256]{1,0:T(4,128)S(1)} collective-permute-done((f32[4,256]{1,0:T(4,128)S(1)}, f32[4,256]{1,0:T(4,128)S(1)}, u32[]{:S(2)}, u32[]{:S(2)}) %collective-permute-start.8) | collective-permute-done | bytes 4128 | tf_op jit(solution)/shard_map/ppermute | solution.py:416
  31.7 0.3 collective-permute-start.10
  32.0 1.4 %collective-permute-start.11 = (f32[4,256]{1,0:T(4,128)S(1)}, f32[4,256]{1,0:T(4,128)S(1)}, u32[]{:S(2)}, u32[]{:S(2)}) collective-permute-start(f32[4,256]{1,0:T(4,128)S(1)} %add.131), channel_id=1, source_target_pairs={{0,7},{1,6},{2,5},{3,4},{4,3},{5,2},{6,1},{7,0},{8,15},{9,14},{10,... | collective-permute-start | bytes 12296 | tf_op jit(solution)/shard_map/ppermute | solution.py:486
  33.4 1.3 %collective-permute-start.9 = (f32[4,256]{1,0:T(4,128)S(1)}, f32[4,256]{1,0:T(4,128)S(1)}, u32[]{:S(2)}, u32[]{:S(2)}) collective-permute-start(f32[4,256]{1,0:T(4,128)S(1)} %add.131), channel_id=1, source_target_pairs={{0,3},{1,2},{2,1},{3,0},{4,7},{5,6},{6,5},{7,4},{8,11},{9,10},{10,... | collective-permute-start | bytes 12296 | tf_op jit(solution)/shard_map/ppermute | solution.py:486
  34.7 0.0 collective-permute-done.10
  34.8 1.2 %collective-permute-done.11 = f32[4,256]{1,0:T(4,128)S(1)} collective-permute-done((f32[4,256]{1,0:T(4,128)S(1)}, f32[4,256]{1,0:T(4,128)S(1)}, u32[]{:S(2)}, u32[]{:S(2)}) %collective-permute-start.11) | collective-permute-done | bytes 4128 | tf_op jit(solution)/shard_map/ppermute | solution.py:486
  36.0 0.5 collective-permute-done.9
  36.5 0.7 collective-permute-start.13
  37.2 3.2 %collective-permute-start.14 = (f32[4,256]{1,0:T(4,128)S(1)}, f32[4,256]{1,0:T(4,128)S(1)}, u32[]{:S(2)}, u32[]{:S(2)}) collective-permute-start(f32[4,256]{1,0:T(4,128)S(1)} %add_add_fusion.1), channel_id=1, source_target_pairs={{0,25},{1,24},{2,27},{3,26},{4,29},{5,28},{6,31},{7,30},{8,17},{9,... | collective-permute-start | bytes 12296 | tf_op jit(solution)/shard_map/ppermute | solution.py:486
  40.4 0.1 collective-permute-done.13
  40.5 1.5 %collective-permute-done.14 = f32[4,256]{1,0:T(4,128)S(1)} collective-permute-done((f32[4,256]{1,0:T(4,128)S(1)}, f32[4,256]{1,0:T(4,128)S(1)}, u32[]{:S(2)}, u32[]{:S(2)}) %collective-permute-start.14) | collective-permute-done | bytes 4128 | tf_op jit(solution)/shard_map/ppermute | solution.py:486
  42.0 4.0 %backward.1 = (bf16[50,96,768]{2,1,0:T(8,128)(2,1)S(1)}, bf16[14,32,768]{2,1,0:T(8,128)(2,1)S(1)}, f32[4,128,256]{2,1,0:T(8,128)S(1)}, bf16[1,4,128,256]{3,2,1,0...) custom-call(bf16[256,4992]{1,0:T(8,128)(2,1)S(1)} %get-tuple-element.84.turned_ref, ...), custom_call_target="tpu_custom_call" | custom-call | flops 3465334016 | bytes 9437184 | tf_op jit(solution)/shard_map/backward/pallas_call | solution.py:700
  46.0 0.3 collective-permute-start.15
  46.3 3.6 %weights.1 = (f32[5,128,256]{2,1,0:T(8,128)S(1)}, bf16[1,5,128,256]{3,2,1,0:T(8,128)(2,1)S(1)}) custom-call(bf16[256,4992]{1,0:T(8,128)(2,1)S(1)} %get-tuple-element.84.turned_ref, bf16[50,96,768]{2,1,0:T(8,128)(2,1)S(1)} %get-tuple-element.120.three_four, bf16[14,32,768]{2,1,0:T(8,128)(2,1)S(1)} %get-tuple-element.96.three_six), custom_call_target="tpu_custom_call" | custom-call | flops 3465334016 | bytes 9437184 | tf_op jit(solution)/shard_map/weights/pallas_call | solution.py:715
  50.0 0.3 collective-permute-start.16
  50.2 0.1 fusion.9
  50.3 1.5 %collective-permute-start.20 = (bf16[128,256]{1,0:T(8,128)(2,1)S(1)}, bf16[128,256]{1,0:T(8,128)(2,1)S(1)}, u32[]{:S(2)}, u32[]{:S(2)}) collective-permute-start(bf16[128,256]{1,0:T(8,128)(2,1)S(1)} %get-tuple-element.152), channel_id=1, source_target_pairs={{0,6},{2,4},{4,2},{6,0},{8,14},{10,12},{12,10},{14,8},{16,22},{18,... | collective-permute-start | bytes 196616 | tf_op jit(solution)/shard_map/ppermute | solution.py:416
  51.8 1.5 %collective-permute-start.21 = (bf16[128,256]{1,0:T(8,128)(2,1)S(1)}, bf16[128,256]{1,0:T(8,128)(2,1)S(1)}, u32[]{:S(2)}, u32[]{:S(2)}) collective-permute-start(bf16[128,256]{1,0:T(8,128)(2,1)S(1)} %get-tuple-element.151), channel_id=1, source_target_pairs={{0,4},{2,6},{4,0},{6,2},{8,12},{10,14},{12,8},{14,10},{16,20},{18,... | collective-permute-start | bytes 196616 | tf_op jit(solution)/shard_map/ppermute | solution.py:416
  53.3 0.5 collective-permute-start.22
  53.9 0.1 fusion.6
  53.9 1.5 %collective-permute-start.17 = (bf16[160,256]{1,0:T(8,128)(2,1)S(1)}, bf16[160,256]{1,0:T(8,128)(2,1)S(1)}, u32[]{:S(2)}, u32[]{:S(2)}) collective-permute-start(bf16[160,256]{1,0:T(8,128)(2,1)S(1)} %get-tuple-element.149), channel_id=1, source_target_pairs={{0,6},{2,4},{4,2},{6,0},{8,14},{10,12},{12,10},{14,8},{16,22},{18,... | collective-permute-start | bytes 245768 | tf_op jit(solution)/shard_map/ppermute | solution.py:416
  55.4 1.5 %collective-permute-start.18 = (bf16[160,256]{1,0:T(8,128)(2,1)S(1)}, bf16[160,256]{1,0:T(8,128)(2,1)S(1)}, u32[]{:S(2)}, u32[]{:S(2)}) collective-permute-start(bf16[160,256]{1,0:T(8,128)(2,1)S(1)} %get-tuple-element.148), channel_id=1, source_target_pairs={{0,4},{2,6},{4,0},{6,2},{8,12},{10,14},{12,8},{14,10},{16,20},{18,... | collective-permute-start | bytes 245768 | tf_op jit(solution)/shard_map/ppermute | solution.py:416
  56.9 0.5 collective-permute-start.19
  57.5 0.7 collective-permute-done.22
  58.2 0.1 collective-permute-start.24
  58.3 2.0 %inputs.2.rest_0_ = bf16[16,96,256]{2,1,0:T(8,128)(2,1)S(1)} custom-call(bf16[50,96,768]{2,1,0:T(8,128)(2,1)S(1)} %get-tuple-element.120.three_four, bf16[2304,256]{1,0:T(8,128)(2,1)S(1)} %get-tuple-element.111.turned), custom_call_target="tpu_custom_call" | custom-call | flops 1732667008 | bytes 1179648 | tf_op jit(solution)/shard_map/inputs/pallas_call | solution.py:734
  60.3 0.3 collective-permute-done.18
  60.6 0.8 collective-permute-done.19
  61.4 0.7 collective-permute-start.23
  62.2 0.4 collective-permute-done.24
  62.6 2.7 %collective-permute-start.27 = (bf16[128,256]{1,0:T(8,128)(2,1)S(1)}, bf16[128,256]{1,0:T(8,128)(2,1)S(1)}, u32[]{:S(2)}, u32[]{:S(2)}) collective-permute-start(bf16[128,256]{1,0:T(8,128)(2,1)S(1)} %add_convert_fusion.6), channel_id=1, source_target_pairs={{0,17},{1,8},{2,19},{3,10},{4,21},{5,12},{6,23},{7,14},{8,1},{9,24... | collective-permute-start | bytes 196616 | tf_op jit(solution)/shard_map/ppermute | solution.py:563
  65.3 2.0 %inputs.3.rest_1_ = bf16[16,96,256]{2,1,0:T(8,128)(2,1)S(1)} custom-call(bf16[50,96,768]{2,1,0:T(8,128)(2,1)S(1)} %get-tuple-element.120.three_four, bf16[2304,256]{1,0:T(8,128)(2,1)S(1)} %get-tuple-element.111.turned), custom_call_target="tpu_custom_call" | custom-call | flops 1732667008 | bytes 1179648 | tf_op jit(solution)/shard_map/inputs/pallas_call | solution.py:734
  67.3 1.2 %collective-permute-start.25 = (bf16[160,256]{1,0:T(8,128)(2,1)S(1)}, bf16[160,256]{1,0:T(8,128)(2,1)S(1)}, u32[]{:S(2)}, u32[]{:S(2)}) collective-permute-start(bf16[160,256]{1,0:T(8,128)(2,1)S(1)} %add_convert_fusion.1), channel_id=1, source_target_pairs={{0,17},{1,8},{2,19},{3,10},{4,21},{5,12},{6,23},{7,14},{8,1},{9,24... | collective-permute-start | bytes 245768 | tf_op jit(solution)/shard_map/ppermute | solution.py:563
  68.6 0.1 collective-permute-start.31
  68.7 1.6 %collective-permute-start.28 = (bf16[128,256]{1,0:T(8,128)(2,1)S(1)}, bf16[128,256]{1,0:T(8,128)(2,1)S(1)}, u32[]{:S(2)}, u32[]{:S(2)}) collective-permute-start(bf16[128,256]{1,0:T(8,128)(2,1)S(1)} %add_convert_fusion.5), channel_id=1, source_target_pairs={{0,6},{1,7},{2,4},{3,5},{4,2},{5,3},{6,0},{7,1},{8,15},{9,14},{10,... | collective-permute-start | bytes 196616 | tf_op jit(solution)/shard_map/ppermute | solution.py:573
  70.2 1.3 %collective-permute-start.29 = (bf16[128,256]{1,0:T(8,128)(2,1)S(1)}, bf16[128,256]{1,0:T(8,128)(2,1)S(1)}, u32[]{:S(2)}, u32[]{:S(2)}) collective-permute-start(bf16[128,256]{1,0:T(8,128)(2,1)S(1)} %add_convert_fusion.5), channel_id=1, source_target_pairs={{0,4},{1,5},{2,6},{3,7},{4,0},{5,1},{6,2},{7,3},{8,13},{9,12},{10,... | collective-permute-start | bytes 196616 | tf_op jit(solution)/shard_map/ppermute | solution.py:573
  71.6 0.6 collective-permute-start.30
  72.3 0.1 collective-permute-start.26
  72.4 1.6 %collective-permute-start.32 = (bf16[160,256]{1,0:T(8,128)(2,1)S(1)}, bf16[160,256]{1,0:T(8,128)(2,1)S(1)}, u32[]{:S(2)}, u32[]{:S(2)}) collective-permute-start(bf16[160,256]{1,0:T(8,128)(2,1)S(1)} %add_convert_fusion), channel_id=1, source_target_pairs={{0,6},{1,7},{2,4},{3,5},{4,2},{5,3},{6,0},{7,1},{8,15},{9,14},{10,... | collective-permute-start | bytes 245768 | tf_op jit(solution)/shard_map/ppermute | solution.py:573
  73.9 1.3 %collective-permute-start.33 = (bf16[160,256]{1,0:T(8,128)(2,1)S(1)}, bf16[160,256]{1,0:T(8,128)(2,1)S(1)}, u32[]{:S(2)}, u32[]{:S(2)}) collective-permute-start(bf16[160,256]{1,0:T(8,128)(2,1)S(1)} %add_convert_fusion), channel_id=1, source_target_pairs={{0,4},{1,5},{2,6},{3,7},{4,0},{5,1},{6,2},{7,3},{8,13},{9,12},{10,... | collective-permute-start | bytes 245768 | tf_op jit(solution)/shard_map/ppermute | solution.py:573
  75.3 0.7 collective-permute-start.34
  76.0 3.3 %inputs_last.1 = (bf16[48,96,256]{2,1,0:T(8,128)(2,1)}, bf16[12,24,256]{2,1,0:T(8,128)(2,1)}) custom-call(bf16[50,96,768]{2,1,0:T(8,128)(2,1)S(1)} %get-tuple-element.120.three_four, bf16[14,32,768]{2,1,0:T(8,128)(2,1)S(1)} %get-tuple-element.96.three_six, bf16[2304,256]{1,0:T(8,128)(2,1)S(1)} %get-tuple-element.111.turned, ...), custom_call_target="tpu_custom_call" | custom-call | flops 2310222592 | bytes 2359296 | tf_op jit(solution)/shard_map/inputs_last/pallas_call | solution.py:778
  79.3 0.6 collective-permute-done.33
  79.9 0.1 broadcast_in_dim.11
  80.3 1.0 %copy-done.7 = f32[36,32,256]{2,1,0:T(8,128)} copy-done((f32[36,32,256]{2,1,0:T(8,128)}, f32[36,32,256]{2,1,0:T(8,128)S(1)}, u32[]{:S(2)}) %copy-start.7) | copy-done | bytes 1179672
  (57 shorter events, 0.5 us)
Async XLA Ops:
  0.7 2.3 %copy-start = (bf16[1,48,96,256]{3,2,1,0:T(8,128)(2,1)S(1)}, bf16[1,48,96,256]{3,2,1,0:T(8,128)(2,1)}, u32[]{:S(2)}) copy-start(bf16[1,48,96,256]{3,2,1,0:T(8,128)(2,1)} %param.7) | copy-start | bytes 7077892
  0.7 2.3 %copy-start.2 = (bf16[9,256,256]{2,1,0:T(8,128)(2,1)S(1)}, bf16[9,256,256]{2,1,0:T(8,128)(2,1)}, u32[]{:S(2)}) copy-start(bf16[9,256,256]{2,1,0:T(8,128)(2,1)} %w_ref.5) | copy-start | bytes 3538948
  0.7 2.3 %copy-start.3 = (bf16[1,12,24,256]{3,2,1,0:T(8,128)(2,1)S(1)}, bf16[1,12,24,256]{3,2,1,0:T(8,128)(2,1)}, u32[]{:S(2)}) copy-start(bf16[1,12,24,256]{3,2,1,0:T(8,128)(2,1)} %param.8) | copy-start | bytes 442372
  2.4 6.4 %collective-permute-start = (bf16[384,256]{1,0:T(8,128)(2,1)}, bf16[384,256]{1,0:T(8,128)(2,1)S(1)}, u32[]{:S(2)}, u32[]{:S(2)}) collective-permute-start(bf16[384,256]{1,0:T(8,128)(2,1)} %edges.1), channel_id=1, source_target_pairs={{0,1},{1,0},{2,3},{3,2},{4,5},{5,4},{6,7},{7,6},{8,9},{9,8},{10,11... | collective-permute-start | bytes 589832 | tf_op jit(solution)/shard_map/ppermute | solution.py:416
  9.6 1.2 %collective-permute-start.1 = (f32[4,256]{1,0:T(4,128)S(1)}, f32[4,256]{1,0:T(4,128)S(1)}, u32[]{:S(2)}, u32[]{:S(2)}) collective-permute-start(f32[4,256]{1,0:T(4,128)S(1)} %get-tuple-element.79), channel_id=1, source_target_pairs={{0,1},{1,0},{2,3},{3,2},{4,5},{5,4},{6,7},{7,6},{8,9},{9,8},{10,11... | collective-permute-start | bytes 12296 | tf_op jit(solution)/shard_map/ppermute | solution.py:416
  10.8 4.0 %collective-permute-start.2 = (f32[4,256]{1,0:T(4,128)S(1)}, f32[4,256]{1,0:T(4,128)S(1)}, u32[]{:S(2)}, u32[]{:S(2)}) collective-permute-start(f32[4,256]{1,0:T(4,128)S(1)} %add.124), channel_id=1, source_target_pairs={{0,3},{1,2},{2,1},{3,0},{4,7},{5,6},{6,5},{7,4},{8,11},{9,10},{10,... | collective-permute-start | bytes 12296 | tf_op jit(solution)/shard_map/ppermute | solution.py:486
  13.4 3.0 %collective-permute-start.3 = (f32[4,256]{1,0:T(4,128)S(1)}, f32[4,256]{1,0:T(4,128)S(1)}, u32[]{:S(2)}, u32[]{:S(2)}) collective-permute-start(f32[4,256]{1,0:T(4,128)S(1)} %add.124), channel_id=1, source_target_pairs={{0,5},{1,4},{2,7},{3,6},{4,1},{5,0},{6,3},{7,2},{8,13},{9,12},{10,... | collective-permute-start | bytes 12296 | tf_op jit(solution)/shard_map/ppermute | solution.py:486
  14.9 3.9 %collective-permute-start.4 = (f32[4,256]{1,0:T(4,128)S(1)}, f32[4,256]{1,0:T(4,128)S(1)}, u32[]{:S(2)}, u32[]{:S(2)}) collective-permute-start(f32[4,256]{1,0:T(4,128)S(1)} %add.124), channel_id=1, source_target_pairs={{0,7},{1,6},{2,5},{3,4},{4,3},{5,2},{6,1},{7,0},{8,15},{9,14},{10,... | collective-permute-start | bytes 12296 | tf_op jit(solution)/shard_map/ppermute | solution.py:486
  18.8 8.8 %copy-start.4 = (bf16[1,12,24,256]{3,2,1,0:T(8,128)(2,1)S(1)}, bf16[1,12,24,256]{3,2,1,0:T(8,128)(2,1)}, u32[]{:S(2)}) copy-start(bf16[1,12,24,256]{3,2,1,0:T(8,128)(2,1)} %param.13) | copy-start | bytes 442372
  18.8 8.8 %copy-start.5 = (f32[2,256]{1,0:T(2,128)S(1)}, f32[2,256]{1,0:T(2,128)}, u32[]{:S(2)}) copy-start(f32[2,256]{1,0:T(2,128)} %gain_ref.3) | copy-start | bytes 6148
  18.8 8.8 %copy-start.6 = (f32[2,256]{1,0:T(2,128)S(1)}, f32[2,256]{1,0:T(2,128)}, u32[]{:S(2)}) copy-start(f32[2,256]{1,0:T(2,128)} %shift_ref.3) | copy-start | bytes 6148
  18.8 5.0 %collective-permute-start.5 = (f32[4,256]{1,0:T(4,128)S(1)}, f32[4,256]{1,0:T(4,128)S(1)}, u32[]{:S(2)}, u32[]{:S(2)}) collective-permute-start(f32[4,256]{1,0:T(4,128)S(1)} %add_add_fusion.3), channel_id=1, source_target_pairs={{0,9},{1,8},{2,11},{3,10},{4,13},{5,12},{6,15},{7,14},{8,1},{9,0},... | collective-permute-start | bytes 12296 | tf_op jit(solution)/shard_map/ppermute | solution.py:486
  20.3 3.9 %collective-permute-start.6 = (f32[4,256]{1,0:T(4,128)S(1)}, f32[4,256]{1,0:T(4,128)S(1)}, u32[]{:S(2)}, u32[]{:S(2)}) collective-permute-start(f32[4,256]{1,0:T(4,128)S(1)} %add_add_fusion.3), channel_id=1, source_target_pairs={{0,17},{1,16},{2,19},{3,18},{4,21},{5,20},{6,23},{7,22},{8,25},{9,... | collective-permute-start | bytes 12296 | tf_op jit(solution)/shard_map/ppermute | solution.py:486
  22.8 4.8 %collective-permute-start.7 = (f32[4,256]{1,0:T(4,128)S(1)}, f32[4,256]{1,0:T(4,128)S(1)}, u32[]{:S(2)}, u32[]{:S(2)}) collective-permute-start(f32[4,256]{1,0:T(4,128)S(1)} %add_add_fusion.3), channel_id=1, source_target_pairs={{0,25},{1,24},{2,27},{3,26},{4,29},{5,28},{6,31},{7,30},{8,17},{9,... | collective-permute-start | bytes 12296 | tf_op jit(solution)/shard_map/ppermute | solution.py:486
  22.8 4.8 %copy-start.1 = (bf16[1,48,96,256]{3,2,1,0:T(8,128)(2,1)S(1)}, bf16[1,48,96,256]{3,2,1,0:T(8,128)(2,1)}, u32[]{:S(2)}) copy-start(bf16[1,48,96,256]{3,2,1,0:T(8,128)(2,1)} %param.12) | copy-start | bytes 7077892
  30.5 1.2 %collective-permute-start.8 = (f32[4,256]{1,0:T(4,128)S(1)}, f32[4,256]{1,0:T(4,128)S(1)}, u32[]{:S(2)}, u32[]{:S(2)}) collective-permute-start(f32[4,256]{1,0:T(4,128)S(1)} %get-tuple-element.92), channel_id=1, source_target_pairs={{0,1},{1,0},{2,3},{3,2},{4,5},{5,4},{6,7},{7,6},{8,9},{9,8},{10,11... | collective-permute-start | bytes 12296 | tf_op jit(solution)/shard_map/ppermute | solution.py:416
  31.7 3.0 %collective-permute-start.10 = (f32[4,256]{1,0:T(4,128)S(1)}, f32[4,256]{1,0:T(4,128)S(1)}, u32[]{:S(2)}, u32[]{:S(2)}) collective-permute-start(f32[4,256]{1,0:T(4,128)S(1)} %add.131), channel_id=1, source_target_pairs={{0,5},{1,4},{2,7},{3,6},{4,1},{5,0},{6,3},{7,2},{8,13},{9,12},{10,... | collective-permute-start | bytes 12296 | tf_op jit(solution)/shard_map/ppermute | solution.py:486
  32.0 3.9 %collective-permute-start.11 = (f32[4,256]{1,0:T(4,128)S(1)}, f32[4,256]{1,0:T(4,128)S(1)}, u32[]{:S(2)}, u32[]{:S(2)}) collective-permute-start(f32[4,256]{1,0:T(4,128)S(1)} %add.131), channel_id=1, source_target_pairs={{0,7},{1,6},{2,5},{3,4},{4,3},{5,2},{6,1},{7,0},{8,15},{9,14},{10,... | collective-permute-start | bytes 12296 | tf_op jit(solution)/shard_map/ppermute | solution.py:486
  33.4 3.0 %collective-permute-start.9 = (f32[4,256]{1,0:T(4,128)S(1)}, f32[4,256]{1,0:T(4,128)S(1)}, u32[]{:S(2)}, u32[]{:S(2)}) collective-permute-start(f32[4,256]{1,0:T(4,128)S(1)} %add.131), channel_id=1, source_target_pairs={{0,3},{1,2},{2,1},{3,0},{4,7},{5,6},{6,5},{7,4},{8,11},{9,10},{10,... | collective-permute-start | bytes 12296 | tf_op jit(solution)/shard_map/ppermute | solution.py:486
  36.5 3.9 %collective-permute-start.12 = (f32[4,256]{1,0:T(4,128)S(1)}, f32[4,256]{1,0:T(4,128)S(1)}, u32[]{:S(2)}, u32[]{:S(2)}) collective-permute-start(f32[4,256]{1,0:T(4,128)S(1)} %add_add_fusion.1), channel_id=1, source_target_pairs={{0,9},{1,8},{2,11},{3,10},{4,13},{5,12},{6,15},{7,14},{8,1},{9,0},... | collective-permute-start | bytes 12296 | tf_op jit(solution)/shard_map/ppermute | solution.py:486
  36.5 4.0 %collective-permute-start.13 = (f32[4,256]{1,0:T(4,128)S(1)}, f32[4,256]{1,0:T(4,128)S(1)}, u32[]{:S(2)}, u32[]{:S(2)}) collective-permute-start(f32[4,256]{1,0:T(4,128)S(1)} %add_add_fusion.1), channel_id=1, source_target_pairs={{0,17},{1,16},{2,19},{3,18},{4,21},{5,20},{6,23},{7,22},{8,25},{9,... | collective-permute-start | bytes 12296 | tf_op jit(solution)/shard_map/ppermute | solution.py:486
  37.2 4.8 %collective-permute-start.14 = (f32[4,256]{1,0:T(4,128)S(1)}, f32[4,256]{1,0:T(4,128)S(1)}, u32[]{:S(2)}, u32[]{:S(2)}) collective-permute-start(f32[4,256]{1,0:T(4,128)S(1)} %add_add_fusion.1), channel_id=1, source_target_pairs={{0,25},{1,24},{2,27},{3,26},{4,29},{5,28},{6,31},{7,30},{8,17},{9,... | collective-permute-start | bytes 12296 | tf_op jit(solution)/shard_map/ppermute | solution.py:486
  46.0 3.9 %collective-permute-start.15 = (bf16[4,128,256]{2,1,0:T(8,128)(2,1)S(1)}, bf16[4,128,256]{2,1,0:T(8,128)(2,1)S(1)}, u32[]{:S(2)}, u32[]{:S(2)}) collective-permute-start(bf16[4,128,256]{2,1,0:T(8,128)(2,1)S(1)} %bitcast.66), channel_id=1, source_target_pairs={{0,1},{1,0},{2,3},{3,2},{4,5},{5,4},{6,7},{7,6},{8,9},{9,8},{10,11... | collective-permute-start | bytes 786440 | tf_op jit(solution)/shard_map/ppermute | solution.py:416
  50.0 3.9 %collective-permute-start.16 = (bf16[5,128,256]{2,1,0:T(8,128)(2,1)S(1)}, bf16[5,128,256]{2,1,0:T(8,128)(2,1)S(1)}, u32[]{:S(2)}, u32[]{:S(2)}) collective-permute-start(bf16[5,128,256]{2,1,0:T(8,128)(2,1)S(1)} %bitcast.65), channel_id=1, source_target_pairs={{0,1},{1,0},{2,3},{3,2},{4,5},{5,4},{6,7},{7,6},{8,9},{9,8},{10,11... | collective-permute-start | bytes 983048 | tf_op jit(solution)/shard_map/ppermute | solution.py:416
  50.3 6.6 %collective-permute-start.20 = (bf16[128,256]{1,0:T(8,128)(2,1)S(1)}, bf16[128,256]{1,0:T(8,128)(2,1)S(1)}, u32[]{:S(2)}, u32[]{:S(2)}) collective-permute-start(bf16[128,256]{1,0:T(8,128)(2,1)S(1)} %get-tuple-element.152), channel_id=1, source_target_pairs={{0,6},{2,4},{4,2},{6,0},{8,14},{10,12},{12,10},{14,8},{16,22},{18,... | collective-permute-start | bytes 196616 | tf_op jit(solution)/shard_map/ppermute | solution.py:416
  51.8 5.7 %collective-permute-start.21 = (bf16[128,256]{1,0:T(8,128)(2,1)S(1)}, bf16[128,256]{1,0:T(8,128)(2,1)S(1)}, u32[]{:S(2)}, u32[]{:S(2)}) collective-permute-start(bf16[128,256]{1,0:T(8,128)(2,1)S(1)} %get-tuple-element.151), channel_id=1, source_target_pairs={{0,4},{2,6},{4,0},{6,2},{8,12},{10,14},{12,8},{14,10},{16,20},{18,... | collective-permute-start | bytes 196616 | tf_op jit(solution)/shard_map/ppermute | solution.py:416
  53.3 4.8 %collective-permute-start.22 = (bf16[128,256]{1,0:T(8,128)(2,1)S(1)}, bf16[128,256]{1,0:T(8,128)(2,1)S(1)}, u32[]{:S(2)}, u32[]{:S(2)}) collective-permute-start(bf16[128,256]{1,0:T(8,128)(2,1)S(1)} %get-tuple-element.150), channel_id=1, source_target_pairs={{0,2},{2,0},{4,6},{6,4},{8,10},{10,8},{12,14},{14,12},{16,18},{18,... | collective-permute-start | bytes 196616 | tf_op jit(solution)/shard_map/ppermute | solution.py:416
  53.9 6.4 %collective-permute-start.17 = (bf16[160,256]{1,0:T(8,128)(2,1)S(1)}, bf16[160,256]{1,0:T(8,128)(2,1)S(1)}, u32[]{:S(2)}, u32[]{:S(2)}) collective-permute-start(bf16[160,256]{1,0:T(8,128)(2,1)S(1)} %get-tuple-element.149), channel_id=1, source_target_pairs={{0,6},{2,4},{4,2},{6,0},{8,14},{10,12},{12,10},{14,8},{16,22},{18,... | collective-permute-start | bytes 245768 | tf_op jit(solution)/shard_map/ppermute | solution.py:416
  55.4 5.2 %collective-permute-start.18 = (bf16[160,256]{1,0:T(8,128)(2,1)S(1)}, bf16[160,256]{1,0:T(8,128)(2,1)S(1)}, u32[]{:S(2)}, u32[]{:S(2)}) collective-permute-start(bf16[160,256]{1,0:T(8,128)(2,1)S(1)} %get-tuple-element.148), channel_id=1, source_target_pairs={{0,4},{2,6},{4,0},{6,2},{8,12},{10,14},{12,8},{14,10},{16,20},{18,... | collective-permute-start | bytes 245768 | tf_op jit(solution)/shard_map/ppermute | solution.py:416
  56.9 4.4 %collective-permute-start.19 = (bf16[160,256]{1,0:T(8,128)(2,1)S(1)}, bf16[160,256]{1,0:T(8,128)(2,1)S(1)}, u32[]{:S(2)}, u32[]{:S(2)}) collective-permute-start(bf16[160,256]{1,0:T(8,128)(2,1)S(1)} %get-tuple-element.147), channel_id=1, source_target_pairs={{0,2},{2,0},{4,6},{6,4},{8,10},{10,8},{12,14},{14,12},{16,18},{18,... | collective-permute-start | bytes 245768 | tf_op jit(solution)/shard_map/ppermute | solution.py:416
  58.2 4.4 %collective-permute-start.24 = (bf16[128,256]{1,0:T(8,128)(2,1)S(1)}, bf16[128,256]{1,0:T(8,128)(2,1)S(1)}, u32[]{:S(2)}, u32[]{:S(2)}) collective-permute-start(bf16[128,256]{1,0:T(8,128)(2,1)S(1)} %fusion.3), channel_id=1, source_target_pairs={{0,9},{1,16},{2,11},{3,18},{4,13},{5,20},{6,15},{7,22},{8,25},{9,0... | collective-permute-start | bytes 196616 | tf_op jit(solution)/shard_map/ppermute | solution.py:563
  61.4 5.8 %collective-permute-start.23 = (bf16[160,256]{1,0:T(8,128)(2,1)S(1)}, bf16[160,256]{1,0:T(8,128)(2,1)S(1)}, u32[]{:S(2)}, u32[]{:S(2)}) collective-permute-start(bf16[160,256]{1,0:T(8,128)(2,1)S(1)} %fusion.1), channel_id=1, source_target_pairs={{0,9},{1,16},{2,11},{3,18},{4,13},{5,20},{6,15},{7,22},{8,25},{9,0... | collective-permute-start | bytes 245768 | tf_op jit(solution)/shard_map/ppermute | solution.py:563
  62.6 6.0 %collective-permute-start.27 = (bf16[128,256]{1,0:T(8,128)(2,1)S(1)}, bf16[128,256]{1,0:T(8,128)(2,1)S(1)}, u32[]{:S(2)}, u32[]{:S(2)}) collective-permute-start(bf16[128,256]{1,0:T(8,128)(2,1)S(1)} %add_convert_fusion.6), channel_id=1, source_target_pairs={{0,17},{1,8},{2,19},{3,10},{4,21},{5,12},{6,23},{7,14},{8,1},{9,24... | collective-permute-start | bytes 196616 | tf_op jit(solution)/shard_map/ppermute | solution.py:563
  67.3 4.9 %collective-permute-start.25 = (bf16[160,256]{1,0:T(8,128)(2,1)S(1)}, bf16[160,256]{1,0:T(8,128)(2,1)S(1)}, u32[]{:S(2)}, u32[]{:S(2)}) collective-permute-start(bf16[160,256]{1,0:T(8,128)(2,1)S(1)} %add_convert_fusion.1), channel_id=1, source_target_pairs={{0,17},{1,8},{2,19},{3,10},{4,21},{5,12},{6,23},{7,14},{8,1},{9,24... | collective-permute-start | bytes 245768 | tf_op jit(solution)/shard_map/ppermute | solution.py:563
  68.6 3.7 %collective-permute-start.31 = (bf16[128,256]{1,0:T(8,128)(2,1)S(1)}, bf16[128,256]{1,0:T(8,128)(2,1)S(1)}, u32[]{:S(2)}, u32[]{:S(2)}) collective-permute-start(bf16[128,256]{1,0:T(8,128)(2,1)S(1)} %add_convert_fusion.5), channel_id=1, source_target_pairs={{0,1},{1,0},{2,3},{3,2},{4,5},{5,4},{6,7},{7,6},{8,9},{9,8},{10,11... | collective-permute-start | bytes 196616 | tf_op jit(solution)/shard_map/ppermute | solution.py:416
  68.7 6.6 %collective-permute-start.28 = (bf16[128,256]{1,0:T(8,128)(2,1)S(1)}, bf16[128,256]{1,0:T(8,128)(2,1)S(1)}, u32[]{:S(2)}, u32[]{:S(2)}) collective-permute-start(bf16[128,256]{1,0:T(8,128)(2,1)S(1)} %add_convert_fusion.5), channel_id=1, source_target_pairs={{0,6},{1,7},{2,4},{3,5},{4,2},{5,3},{6,0},{7,1},{8,15},{9,14},{10,... | collective-permute-start | bytes 196616 | tf_op jit(solution)/shard_map/ppermute | solution.py:573
  70.2 9.1 %collective-permute-start.29 = (bf16[128,256]{1,0:T(8,128)(2,1)S(1)}, bf16[128,256]{1,0:T(8,128)(2,1)S(1)}, u32[]{:S(2)}, u32[]{:S(2)}) collective-permute-start(bf16[128,256]{1,0:T(8,128)(2,1)S(1)} %add_convert_fusion.5), channel_id=1, source_target_pairs={{0,4},{1,5},{2,6},{3,7},{4,0},{5,1},{6,2},{7,3},{8,13},{9,12},{10,... | collective-permute-start | bytes 196616 | tf_op jit(solution)/shard_map/ppermute | solution.py:573
  71.6 7.7 %collective-permute-start.30 = (bf16[128,256]{1,0:T(8,128)(2,1)S(1)}, bf16[128,256]{1,0:T(8,128)(2,1)S(1)}, u32[]{:S(2)}, u32[]{:S(2)}) collective-permute-start(bf16[128,256]{1,0:T(8,128)(2,1)S(1)} %add_convert_fusion.5), channel_id=1, source_target_pairs={{0,2},{1,3},{2,0},{3,1},{4,6},{5,7},{6,4},{7,5},{8,11},{9,10},{10,... | collective-permute-start | bytes 196616 | tf_op jit(solution)/shard_map/ppermute | solution.py:573
  72.3 1.7 %collective-permute-start.26 = (bf16[160,256]{1,0:T(8,128)(2,1)S(1)}, bf16[160,256]{1,0:T(8,128)(2,1)S(1)}, u32[]{:S(2)}, u32[]{:S(2)}) collective-permute-start(bf16[160,256]{1,0:T(8,128)(2,1)S(1)} %add_convert_fusion), channel_id=1, source_target_pairs={{0,1},{1,0},{2,3},{3,2},{4,5},{5,4},{6,7},{7,6},{8,9},{9,8},{10,11... | collective-permute-start | bytes 245768 | tf_op jit(solution)/shard_map/ppermute | solution.py:416
  72.4 7.0 %collective-permute-start.32 = (bf16[160,256]{1,0:T(8,128)(2,1)S(1)}, bf16[160,256]{1,0:T(8,128)(2,1)S(1)}, u32[]{:S(2)}, u32[]{:S(2)}) collective-permute-start(bf16[160,256]{1,0:T(8,128)(2,1)S(1)} %add_convert_fusion), channel_id=1, source_target_pairs={{0,6},{1,7},{2,4},{3,5},{4,2},{5,3},{6,0},{7,1},{8,15},{9,14},{10,... | collective-permute-start | bytes 245768 | tf_op jit(solution)/shard_map/ppermute | solution.py:573
  73.9 6.0 %collective-permute-start.33 = (bf16[160,256]{1,0:T(8,128)(2,1)S(1)}, bf16[160,256]{1,0:T(8,128)(2,1)S(1)}, u32[]{:S(2)}, u32[]{:S(2)}) collective-permute-start(bf16[160,256]{1,0:T(8,128)(2,1)S(1)} %add_convert_fusion), channel_id=1, source_target_pairs={{0,4},{1,5},{2,6},{3,7},{4,0},{5,1},{6,2},{7,3},{8,13},{9,12},{10,... | collective-permute-start | bytes 245768 | tf_op jit(solution)/shard_map/ppermute | solution.py:573
  75.3 4.6 %collective-permute-start.34 = (bf16[160,256]{1,0:T(8,128)(2,1)S(1)}, bf16[160,256]{1,0:T(8,128)(2,1)S(1)}, u32[]{:S(2)}, u32[]{:S(2)}) collective-permute-start(bf16[160,256]{1,0:T(8,128)(2,1)S(1)} %add_convert_fusion), channel_id=1, source_target_pairs={{0,2},{1,3},{2,0},{3,1},{4,6},{5,7},{6,4},{7,5},{8,11},{9,10},{10,... | collective-permute-start | bytes 245768 | tf_op jit(solution)/shard_map/ppermute | solution.py:573
  80.3 1.0 %copy-start.7 = (f32[36,32,256]{2,1,0:T(8,128)}, f32[36,32,256]{2,1,0:T(8,128)S(1)}, u32[]{:S(2)}) copy-start(f32[36,32,256]{2,1,0:T(8,128)S(1)} %convert_dynamic-update-slice_fusion) | copy-start | bytes 3538948
